TPU v7x, 128 devices: a whole 4x4x4 slice. The times are simulated.
128 devices in a mesh: band: 16 (over x_lo, y, core), dom: 8 (over z, x_hi).
Axes of the slice: x: 4 (x_hi: 2, x_lo: 2; x = x_hi * 2 + x_lo), y: 4, z: 4, core: 2. Of those that a mesh axis runs over, the one named last changes fastest.
Arguments:
- orbitals: bfloat16 [384, 48, 6144], P('band', 'dom'), may hold values from -6 to 6
- potential: float32 [48, 6144], P('dom', 'band'), may hold values from -3 to 1
Outputs:
- subspace: float32 [384, 384], P('band')
All inputs are finite; a program needn't handle non-finite values.
Results may differ from a plain program's by a relative error of at most 0.0003.
Values may be sent and summed in bfloat16 or wider, within the bound.
No kernel may reach another device: no remote copies, remote signals or barrier semaphores. Data moves between devices by JAX's collectives and lax.ppermute only.
A program may use at most 256 MiB of HBM per device.

v0:
```python
import jax
import jax.numpy as jnp
from jax import lax
from jax.sharding import PartitionSpec as P

NZ = 64


STENCIL = (
    -5369.0 / 1800.0,
    12.0 / 7.0,
    -15.0 / 56.0,
    10.0 / 189.0,
    -1.0 / 112.0,
    2.0 / 1925.0,
    -1.0 / 16632.0,
)


def padded(cells, sides, width):
    for axis, dim in sides:
        count = lax.axis_size(axis)
        head = lax.slice_in_dim(cells, 0, width, axis=dim)
        tail = lax.slice_in_dim(cells, cells.shape[dim] - width, cells.shape[dim], axis=dim)
        cells = jnp.concatenate(
            [
                lax.ppermute(tail, axis, [(i, (i + 1) % count) for i in range(count)]),
                cells,
                lax.ppermute(head, axis, [((i + 1) % count, i) for i in range(count)]),
            ],
            axis=dim,
        )
    return cells


def contract(left, right):
    return lax.dot_general(
        left, right, (((1,), (1,)), ((), ())), preferred_element_type=jnp.float32
    )


def per_device(orbitals, potential):
    bands_dev = orbitals.shape[0]
    third_cells = NZ
    cells_all = orbitals.shape[1] * lax.axis_size("dom") * orbitals.shape[2]
    field = lax.all_gather(potential, "band", axis=1, tiled=True)
    span_x = orbitals.shape[1]
    span_flat = orbitals.shape[2]
    padded_x = padded(orbitals, (("dom", 1),), 6)
    center = orbitals.astype(jnp.float32)
    third_index = lax.broadcasted_iota(jnp.int32, (1, 1, span_flat), 2) % third_cells
    laplace = 3.0 * STENCIL[0] * center
    for offset in range(1, 7):
        along_x = padded_x[:, 6 + offset : 6 + offset + span_x].astype(jnp.float32) + padded_x[
            :, 6 - offset : 6 - offset + span_x
        ].astype(jnp.float32)
        minus_z = jnp.where(
            third_index >= offset,
            jnp.roll(center, offset, 2),
            jnp.roll(center, offset - third_cells, 2),
        )
        plus_z = jnp.where(
            third_index < third_cells - offset,
            jnp.roll(center, -offset, 2),
            jnp.roll(center, third_cells - offset, 2),
        )
        laplace = laplace + STENCIL[offset] * (
            along_x
            + (
                jnp.roll(center, offset * third_cells, 2)
                + jnp.roll(center, -offset * third_cells, 2)
            )
            + minus_z
            + plus_z
        )
    applied = (-0.5 * laplace + field[None] * center).astype(jnp.bfloat16)
    own_rows = orbitals.reshape(bands_dev, -1)
    block_in = lax.all_gather(applied, "band", axis=0, tiled=True)
    width_now = block_in.shape[0]
    product = contract(own_rows, block_in.reshape(width_now, -1))
    tile_rows = product
    tile_rows = lax.psum(tile_rows, "dom")
    scaling = 1.0 / jnp.sqrt(jnp.float32(cells_all))
    return tile_rows * scaling


def solution(mesh):
    placed = (P("band", "dom", None), P("dom", "band"))
    return jax.shard_map(
        per_device, mesh=mesh, in_specs=placed, out_specs=P("band", None), check_vma=False
    )
```

profile of v0, /device:TPU:0, one launch (start us, length us, event | category | flops | bytes accessed | tf_op | source)
XLA Modules:
  0.0 370.1 jit_solution(2341360805954748604)
XLA Ops:
  6.5 0.0 copy-start
  6.5 0.0 all-gather.2.cloned.1.call-start
  6.5 3.1 collective-permute-start.1
  9.6 3.5 collective-permute-start
  13.2 0.6 fusion.37
  13.8 0.6 fusion.35
  14.4 1.5 fusion.59
  15.9 1.5 fusion.68
  17.4 1.5 fusion.71
  18.9 1.5 fusion.56
  20.4 1.5 fusion.65
  21.9 1.5 fusion.54
  23.3 1.5 fusion.74
  24.8 1.5 fusion.77
  26.3 1.5 fusion.62
  27.8 1.5 fusion.53
  29.3 1.5 fusion.80
  30.8 1.5 fusion.83
  32.3 0.0 copy-done
  32.3 0.7 fusion.50
  33.0 0.7 fusion.48
  33.8 0.7 fusion.60
  34.5 0.7 fusion.66
  35.2 0.1 fusion.72
  35.4 3.1 fusion.79
  38.4 3.4 fusion.73
  41.8 3.2 fusion.67
  45.1 3.4 fusion.55
  48.4 3.4 fusion.61
  51.8 2.7 fusion.58
  54.5 3.7 %fusion.69 = (f32[24,6,6140]{2,0,1:T(8,128)}, f32[24,6,6140]{2,0,1:T(8,128)}) fusion(bf16[24,6,6144]{2,0,1:T(8,128)(2,1)S(1)} %copy-done), kind=kLoop, calls=%fused_computation.95 | loop fusion | bytes 14146560 | tf_op jit(solution)/shard_map/jit(_roll_static)/slice | solution.py:59
  58.2 3.6 fusion.70
  61.8 3.7 %fusion.57 = (f32[24,6,6142]{2,0,1:T(8,128)}, f32[24,6,6142]{2,0,1:T(8,128)}) fusion(bf16[24,6,6144]{2,0,1:T(8,128)(2,1)S(1)} %copy-done), kind=kLoop, calls=%fused_computation.83 | loop fusion | bytes 14151168 | tf_op jit(solution)/shard_map/jit(_roll_static)/slice | solution.py:59
  65.5 3.5 fusion.64
  69.0 3.7 fusion.75
  72.7 3.6 fusion.76
  76.3 3.6 fusion.63
  79.9 3.5 fusion.52
  83.4 3.7 %fusion.81 = (f32[24,6,6138]{2,0,1:T(8,128)}, f32[24,6,6138]{2,0,1:T(8,128)}) fusion(bf16[24,6,6144]{2,0,1:T(8,128)(2,1)S(1)} %copy-done), kind=kLoop, calls=%fused_computation.107 | loop fusion | bytes 14141952 | tf_op jit(solution)/shard_map/jit(_roll_static)/slice | solution.py:59
  87.2 3.5 fusion.82
  90.7 3.8 %fusion.51 = (f32[24,6,6143]{2,0,1:T(8,128)}, f32[24,6,6143]{2,0,1:T(8,128)}) fusion(bf16[24,6,6144]{2,0,1:T(8,128)(2,1)S(1)} %copy-done), kind=kLoop, calls=%fused_computation.77 | loop fusion | bytes 14153472 | tf_op jit(solution)/shard_map/jit(_roll_static)/slice | solution.py:59
  94.6 0.0 copy-start.2
  94.6 3.7 fusion.49
  98.2 0.0 copy-done.2
  98.2 20.9 %all_gather.6 = f32[6,6144]{1,0:T(8,128)} all-gather(f32[6,384]{1,0:T(8,128)S(1)} %copy-done.2), channel_id=1, replica_groups=mesh['band'=16,'dom'=8] {'band'}, dimensions={1}, use_global_device_ids=true | all-gather | bytes 156672 | tf_op jit(solution)/shard_map/all_gather | solution.py:46
  119.1 0.8 fusion.78
  120.0 0.0 collective-permute-done.1
  120.0 0.2 constant_dynamic-update-slice_fusion.3
  120.1 0.5 constant_dynamic-update-slice_fusion.1
  120.6 0.0 collective-permute-done
  120.6 0.0 copy-start.1
  120.6 0.1 constant_dynamic-update-slice_fusion
  120.8 1.1 copy-done.1
  121.8 41.9 %fusion.32 = bf16[24,6,6144]{2,0,1:T(8,128)(2,1)} fusion(f32[24,6,6086]{2,0,1:T(8,128)} %get-tuple-element.76, f32[24,6,58]{2,0,1:T(8,128)} %get-tuple-element.78, f32[24,6,6]{2,0,1:T(8,128)} %get-tuple-element.72, f32[24,6,6138]{2,0,1:T(8,128)} %get-tuple-element.74, f32[24,6,58]{2,0,1:T(8,128)} %get-tuple-element.77, f32[24,6,6086]{2,0,1:T(8,128)} %get-tuple-element.75, ...), kind=kLoop, calls=%fused_computation.50 | loop fusion | flops 95551488 | bytes 152395776 | tf_op jit(solution)/shard_map/convert_element_type | solution.py:76
  163.8 0.0 all-gather.2.cloned.1.call-update
  163.8 143.4 %all-gather.2.cloned.1.call-done = bf16[384,6,6144]{2,0,1:T(8,128)(2,1)} async-done(((bf16[24,6,6144]{2,0,1:T(8,128)(2,1)}), bf16[384,6,6144]{2,0,1:T(8,128)(2,1)}) %all-gather.2.cloned.1.call-update) | async-done | bytes 28311568 | tf_op jit(solution)/shard_map/all_gather | solution.py:78
  307.2 12.8 %convolution_bitcast_fusion = f32[24,384]{1,0:T(8,128)S(1)} fusion(bf16[384,6,6144]{2,0,1:T(8,128)(2,1)} %all-gather.2.cloned.1.call-done, bf16[24,6,6144]{2,0,1:T(8,128)(2,1)S(1)} %copy-done), kind=kOutput, calls=%fused_computation.51 | convolution fusion | flops 679477248 | bytes 30117888 | tf_op jit(solution)/shard_map/dot_general | solution.py:37
  320.1 42.5 %psum.7 = f32[24,384]{1,0:T(8,128)S(1)} all-reduce(f32[24,384]{1,0:T(8,128)S(1)} %convolution_bitcast_fusion), channel_id=1, replica_groups=mesh['band'=16,'dom'=8] {'dom'}, use_global_device_ids=true, to_apply=%region_0.1 | all-reduce | flops 9216 | bytes 73728 | tf_op jit(solution)/shard_map/psum | solution.py:82
  362.6 0.6 broadcast_multiply_fusion
  (4 shorter events, 0.1 us)
Async XLA Ops:
  6.5 25.8 %copy-start = (bf16[24,6,6144]{2,0,1:T(8,128)(2,1)S(1)}, bf16[24,6,6144]{2,0,1:T(8,128)(2,1)}, u32[]{:S(2)}) copy-start(bf16[24,6,6144]{2,0,1:T(8,128)(2,1)} %param.2) | copy-start | bytes 5308420
  6.5 300.7 %all-gather.2.cloned.1.call-start = ((), (), s32[]{:S(2)}) async-start(), calls=%async_computation | async-start | bytes 30081024 | tf_op jit(solution)/shard_map/all_gather | solution.py:78
  6.5 113.4 %collective-permute-start.1 = (bf16[24,6,6144]{2,0,1:T(8,128)(2,1)}, bf16[24,6,6144]{2,0,1:T(8,128)(2,1)S(1)}, u32[]{:S(2)}, u32[]{:S(2)}) collective-permute-start(bf16[24,6,6144]{2,0,1:T(8,128)(2,1)} %param.2), channel_id=1, source_target_pairs={{0,1},{1,2},{2,3},{3,4},{4,5},{5,6},{6,7},{7,0},{8,9},{9,10},{10,1... | collective-permute-start | bytes 5308424 | tf_op jit(solution)/shard_map/ppermute | solution.py:27
  9.6 111.0 %collective-permute-start = (bf16[24,6,6144]{2,0,1:T(8,128)(2,1)}, bf16[24,6,6144]{2,0,1:T(8,128)(2,1)S(1)}, u32[]{:S(2)}, u32[]{:S(2)}) collective-permute-start(bf16[24,6,6144]{2,0,1:T(8,128)(2,1)} %param.2), channel_id=1, source_target_pairs={{1,0},{2,1},{3,2},{4,3},{5,4},{6,5},{7,6},{0,7},{9,8},{10,9},{11,1... | collective-permute-start | bytes 5308424 | tf_op jit(solution)/shard_map/ppermute | solution.py:29
  94.6 3.7 copy-start.2
  120.6 1.2 copy-start.1
Sparse Core Ops, SparseCore 0:
  163.9 143.2 all-gather.1
where the time goes:
time: 371 us; the launch traced here: 370 us
  waiting for transfers between devices  143 us (39%)
  local copies, waits for them, and re-layouts  86.5 us (23%)
  blocking collectives  63.4 us (17%)
  other arithmetic  43.8 us (12%)
  between operations  13.5 us (4%)
  matrix products  12.8 us (3%)
  starting transfers between devices  6.59 us (2%)
    all_gather x1, waiting for transfers between devices, per_device(): block_in = lax.all_gather(applied, 'band', axis=0, tiled=True)  143 us
    psum x1, blocking collectives, per_device(): tile_rows = lax.psum(tile_rows, 'dom')  42.5 us
    convert_element_type x1, other arithmetic, per_device(): applied = (-0.5 * laplace + field[None] * center).astype(jnp.bfloat16)  41.9 us
    slice x12, local copies, waits for them, and re-layouts, per_device(): jnp.roll(center, offset, 2)  30.6 us
    slice x12, local copies, waits for them, and re-layouts, per_device(): jnp.roll(center, offset - third_cells, 2)  29.3 us
    slice x12, local copies, waits for them, and re-layouts, per_device(): jnp.roll(center, offset * third_cells, 2)  24.7 us
    all_gather x1, blocking collectives, per_device(): field = lax.all_gather(potential, 'band', axis=1, tiled=True)  20.9 us
    dot_general x1, matrix products, contract(): lax.dot_general(left, right, (((1,), (1,)), ((), ())), preferred_element_...  12.8 us
  transfers between devices with their start and end apart: 3, of which 1 were waited for; matrix products, arithmetic and copies ran while one was open for 23% of the time, Pallas kernels for 0%

commit v1 on v0

v1 whole, which is shorter than its diff:
```python
import functools
import math

import jax
import jax.numpy as jnp
import ml_dtypes
import numpy as np
from jax import lax
from jax.experimental import pallas as pl
from jax.experimental.pallas import tpu as pltpu
from jax.sharding import PartitionSpec as P

NZ = 64
LANES = 128
BLOCKS = 8
WIDTH = LANES // BLOCKS
REACH = 6


STENCIL = (
    -5369.0 / 1800.0,
    12.0 / 7.0,
    -15.0 / 56.0,
    10.0 / 189.0,
    -1.0 / 112.0,
    2.0 / 1925.0,
    -1.0 / 16632.0,
)


def halves(matrix):
    high = matrix.astype(ml_dtypes.bfloat16)
    low = (matrix - high.astype(np.float64)).astype(ml_dtypes.bfloat16)
    return jnp.asarray(np.stack([high, low]))


def upward_plane(cells):
    matrix = np.zeros((2 * cells, cells))
    out = np.arange(cells)
    matrix[out, out] = -0.75 * STENCIL[0]
    for k in range(1, REACH + 1):
        matrix[out + k * NZ, out] += -0.5 * STENCIL[k]
        matrix[out // NZ * NZ + (out + k) % NZ, out] += -0.5 * STENCIL[k]
    return halves(matrix)


def upward_next(layers, rows):
    matrix = np.zeros((3 * LANES, 3 * LANES))
    for x in range(layers):
        for k in range(1, REACH + 1):
            there = x + k - layers
            if 0 <= there < layers:
                for v in range(rows):
                    for j in range(WIDTH):
                        matrix[(there * rows + v) * WIDTH + j, (x * rows + v) * WIDTH + j] = -0.5 * STENCIL[k]
    return halves(matrix)


def spread_matrix():
    matrix = np.zeros((LANES, 3 * LANES), ml_dtypes.bfloat16)
    for piece in range(3):
        for j in range(WIDTH):
            matrix[LANES // 2 + piece * WIDTH + j, j::WIDTH] = 1.0
    return jnp.asarray(matrix)


def exchange_blocks(tiles):
    lane = lax.broadcasted_iota(jnp.int32, tiles[0].shape, 1)
    for bit in (4, 2, 1):
        upper = (lane // (bit * WIDTH)) % 2 == 1
        moved = list(tiles)
        for i in range(BLOCKS):
            if not i & bit:
                a, b = tiles[i], tiles[i | bit]
                moved[i] = jnp.where(upper, pltpu.roll(b, bit * WIDTH, 1), a)
                moved[i | bit] = jnp.where(upper, b, pltpu.roll(a, LANES - bit * WIDTH, 1))
        tiles = moved
    return tiles


def apply_kernel(layers, bands, here_ref, next_ref, plane_ref, potential_ref, out_ref):
    here = here_ref[...]
    both = jnp.concatenate([here, next_ref[...]], axis=1)
    applied = jnp.dot(both, plane_ref[0], preferred_element_type=jnp.float32) + jnp.dot(
        both, plane_ref[1], preferred_element_type=jnp.float32
    )
    center = here.astype(jnp.float32)
    rows = here.shape[1] // LANES
    psi, half = [], []
    for x in range(layers):
        total = applied[x * bands : (x + 1) * bands]
        for k in range(1, layers - x):
            total = total + (-0.5 * STENCIL[k]) * center[(x + k) * bands : (x + k + 1) * bands]
        for v in range(rows):
            psi.append(center[x * bands : (x + 1) * bands, v * LANES : (v + 1) * LANES])
            half.append(total[:, v * LANES : (v + 1) * LANES])
    field = potential_ref[...]
    pieces = []
    for _ in range(3):
        piece = field.astype(jnp.bfloat16).astype(jnp.float32)
        pieces.append(piece)
        field = field - piece
    groups = [psi[:8], psi[8:16], half[:8], half[8:16], psi[16:] + half[16:] + pieces + [jnp.zeros_like(field)]]
    groups = [exchange_blocks(group) for group in groups]
    for there in range(BLOCKS):
        out_ref[there] = jnp.concatenate([group[there] for group in groups], axis=0).astype(jnp.bfloat16)


def product_kernel(bands, scaling, own_ref, blocks_ref, next_plane_ref, spread_ref, out_ref, total, after):
    step = pl.program_id(0)
    count = blocks_ref.shape[0]
    size = count * bands

    def group(at):
        return blocks_ref[:, 0, at * bands : (at + 1) * bands, :].astype(jnp.float32).reshape(size, LANES)

    psi_first, psi_second, rest = group(0), group(1), group(4)
    psi = jnp.concatenate([psi_first, psi_second, rest], axis=1)
    psi_sent = psi.astype(jnp.bfloat16)

    @pl.when(step == 0)
    def _():
        total[...] = jnp.zeros_like(total)

    @pl.when(step > 0)
    def _():
        beyond = jnp.dot(after[...], next_plane_ref[0], preferred_element_type=jnp.float32) + jnp.dot(
            after[...], next_plane_ref[1], preferred_element_type=jnp.float32
        )
        own = blocks_ref[own_ref[0], 0, 4 * bands : 5 * bands, :]
        field = jnp.dot(own, spread_ref[...], preferred_element_type=jnp.float32)
        row = lax.broadcasted_iota(jnp.int32, field.shape, 0)
        lane = lax.broadcasted_iota(jnp.int32, field.shape, 1)
        field = jnp.sum(jnp.where(lane // WIDTH == row, field, 0.0), axis=0, keepdims=True)
        rest_lane = lax.broadcasted_iota(jnp.int32, rest.shape, 1)
        half_rest = jnp.where(rest_lane < 2 * WIDTH, pltpu.roll(rest, LANES - 2 * WIDTH, 1), 0.0)
        half = jnp.concatenate([group(2), group(3), half_rest], axis=1)
        half = half + beyond + (0.5 * field) * psi
        total[...] += lax.dot_general(
            psi_sent, half.astype(jnp.bfloat16), (((1,), (1,)), ((), ())), preferred_element_type=jnp.float32
        )

    after[...] = psi_sent

    @pl.when(step == pl.num_programs(0) - 1)
    def _():
        whole = total[...] * scaling
        out_ref[...] = whole + whole.T


def per_device(orbitals, potential):
    bands, layers, cells_row = orbitals.shape
    count = lax.axis_size("band")
    doms = lax.axis_size("dom")
    cells = cells_row // count
    rows = cells // LANES
    chunk = 5 * bands
    size = count * bands
    cells_all = layers * doms * cells_row
    planes = jnp.transpose(orbitals, (1, 0, 2)).reshape(layers * bands, cells_row)
    field = jnp.pad(potential.reshape(layers * rows, LANES), ((0, bands - layers * rows), (0, 0)))
    packed = pl.pallas_call(
        functools.partial(apply_kernel, layers, bands),
        grid=(count,),
        in_specs=[
            pl.BlockSpec((layers * bands, cells), lambda i: (0, i)),
            pl.BlockSpec((layers * bands, cells), lambda i: (0, (i + 1) % count)),
            pl.BlockSpec((2, 2 * cells, cells), lambda i: (0, 0, 0)),
            pl.BlockSpec((bands, LANES), lambda i: (0, 0)),
        ],
        out_specs=pl.BlockSpec((doms, chunk, LANES), lambda i: (i, 0, 0)),
        out_shape=jax.ShapeDtypeStruct((count * doms, chunk, LANES), jnp.bfloat16),
        compiler_params=pltpu.CompilerParams(vmem_limit_bytes=32 * 2**20),
        name="apply_upward",
    )(planes, planes, upward_plane(cells), field)
    received = lax.all_to_all(packed, ("band", "dom"), 0, 0, tiled=True)
    partial = pl.pallas_call(
        functools.partial(product_kernel, bands, 1.0 / math.sqrt(cells_all)),
        grid=(doms + 1,),
        in_specs=[
            pl.BlockSpec(memory_space=pltpu.SMEM),
            pl.BlockSpec((count, 1, chunk, LANES), lambda i: (0, (doms - i) % doms, 0, 0)),
            pl.BlockSpec((2, 3 * LANES, 3 * LANES), lambda i: (0, 0, 0)),
            pl.BlockSpec((LANES, 3 * LANES), lambda i: (0, 0)),
        ],
        out_specs=pl.BlockSpec((size, size), lambda i: (0, 0)),
        out_shape=jax.ShapeDtypeStruct((size, size), jnp.float32),
        scratch_shapes=[
            pltpu.VMEM((size, size), jnp.float32),
            pltpu.VMEM((size, 3 * LANES), jnp.bfloat16),
        ],
        compiler_params=pltpu.CompilerParams(vmem_limit_bytes=32 * 2**20),
        name="subspace_product",
    )(
        lax.axis_index("band").astype(jnp.int32).reshape(1),
        received.reshape(count, doms, chunk, LANES),
        upward_next(layers, rows),
        spread_matrix(),
    )
    own_rows = lax.all_to_all(partial.reshape(count, bands, size), "band", 0, 0, tiled=True).sum(0)
    copies = jnp.broadcast_to(own_rows, (doms, bands, size))
    return lax.all_to_all(copies, "dom", 0, 0, tiled=True).sum(0)


def solution(mesh):
    placed = (P("band", "dom", None), P("dom", "band"))
    return jax.shard_map(
        per_device, mesh=mesh, in_specs=placed, out_specs=P("band", None), check_vma=False
    )
```

time: 371 us -> 116 us (0.31)
  waiting for transfers between devices: 143 us -> 48.8 us
  local copies, waits for them, and re-layouts: 86.5 us -> 5.39 us
  other arithmetic: 43.8 us -> 0.67 us
  blocking collectives: 63.4 us -> 27.4 us
  Pallas kernels: 0 us -> 21.7 us
  between operations: 13.5 us -> 0.05 us
  matrix products: 12.8 us -> 0 us
  starting transfers between devices: 6.59 us -> 11.6 us
    all_gather x1 -> x0, waiting for transfers between devices: 143 us -> none  [per_device(): block_in = lax.all_gather(applied, 'band', axis=0, tiled=True)]
    slice x36 -> x0, local copies, waits for them, and re-layouts: 84.6 us -> none  [the longest x12 30.6 us: per_device(): jnp.roll(center, offset, 2)]
    all_to_all x0 -> x1, waiting for transfers between devices: none -> 48.8 us  [per_device(): received = lax.all_to_all(packed, ('band', 'dom'), 0, 0, tiled=True)]
    psum x1 -> x0, blocking collectives: 42.5 us -> none  [per_device(): tile_rows = lax.psum(tile_rows, 'dom')]
    convert_element_type x1 -> x0, other arithmetic: 41.9 us -> none  [per_device(): applied = (-0.5 * laplace + field[None] * center).astype(jnp.bfloat16)]
    all_to_all x0 -> x2, blocking collectives: none -> 27.4 us  [the longest x1 14.9 us: per_device(): lax.all_to_all(partial.reshape(count, bands, size), 'band', 0, 0, tiled=T...]
    pallas_call x0 -> x2, Pallas kernels: none -> 21.7 us  [the longest x1 12.1 us: per_device(): pl.pallas_call(functools.partial(apply_kernel, layers, bands), grid=(coun...]
    all_gather x1 -> x0, blocking collectives: 20.9 us -> none  [per_device(): field = lax.all_gather(potential, 'band', axis=1, tiled=True)]
  transfers between devices with their start and end apart: 3 -> 1, of which waited for: 1 -> 1; matrix products, arithmetic and copies ran while one was open for 23% -> 0% of each run, Pallas kernels for 0% -> 0%
where the time goes in v1:
time: 116 us
  waiting for transfers between devices  48.8 us (42%)
  blocking collectives  27.4 us (24%)
  Pallas kernels  21.7 us (19%)
  starting transfers between devices  11.6 us (10%)
  local copies, waits for them, and re-layouts  5.39 us (5%)
    all_to_all x1, waiting for transfers between devices, per_device(): received = lax.all_to_all(packed, ('band', 'dom'), 0, 0, tiled=True)  48.8 us
    all_to_all x1, blocking collectives, per_device(): lax.all_to_all(partial.reshape(count, bands, size), 'band', 0, 0, tiled=T...  14.9 us
    all_to_all x1, blocking collectives, per_device(): return lax.all_to_all(copies, 'dom', 0, 0, tiled=True).sum(0)  12.6 us
    pallas_call x1, Pallas kernels, per_device(): pl.pallas_call(functools.partial(apply_kernel, layers, bands), grid=(coun...  12.1 us
    all_to_all x1, starting transfers between devices, per_device(): received = lax.all_to_all(packed, ('band', 'dom'), 0, 0, tiled=True)  11.6 us
    pallas_call x1, Pallas kernels, per_device(): pl.pallas_call(functools.partial(product_kernel, bands, 1.0 / math.sqrt(c...  9.62 us
    unnamed x10, local copies, waits for them, and re-layouts  4.65 us
  transfers between devices with their start and end apart: 1, of which 1 were waited for; matrix products, arithmetic and copies ran while one was open for 0% of the time, Pallas kernels for 0%

profile of v1, /device:TPU:0, one launch (start us, length us, event | category | flops | bytes accessed | tf_op | source)
XLA Modules:
  0.0 115.6 jit_solution(9501202809625851928)
XLA Ops:
  0.0 0.7 reshape.17
  0.7 0.0 copy-start.1
  0.7 1.5 %copy-done.1 = bf16[24,6,6144]{2,0,1:T(8,128)(2,1)S(1)} copy-done((bf16[24,6,6144]{2,0,1:T(8,128)(2,1)S(1)}, bf16[24,6,6144]{2,0,1:T(8,128)(2,1)}, u32[]{:S(2)}) %copy-start.1) | copy-done | bytes 1769496
  2.2 0.0 copy-start.2
  2.2 1.3 %copy-done.2 = bf16[2,768,384]{2,1,0:T(8,128)(2,1)S(1)} copy-done((bf16[2,768,384]{2,1,0:T(8,128)(2,1)S(1)}, bf16[2,768,384]{2,1,0:T(8,128)(2,1)}, u32[]{:S(2)}) %copy-start.2) | copy-done | bytes 1179672
  3.5 12.1 %apply_upward.1 = bf16[128,120,128]{2,1,0:T(8,128)(2,1)S(1)} custom-call(bf16[144,6144]{1,0:T(8,128)(2,1)S(1)} %bitcast.6, bf16[144,6144]{1,0:T(8,128)(2,1)S(1)} %bitcast.7, bf16[2,768,384]{2,1,0:T(8,128)(2,1)S(1)} %copy-done.2, f32[24,128]{1,0:T(8,128)S(1)} %pad.4.potential_ref), custom_call_target="tpu_custom_call" | custom-call | tf_op jit(solution)/shard_map/apply_upward/pallas_call | solution.py:162
  15.6 0.0 copy-start
  15.6 1.9 %copy-done = bf16[128,120,128]{2,1,0:T(8,128)(2,1)} copy-done((bf16[128,120,128]{2,1,0:T(8,128)(2,1)}, bf16[128,120,128]{2,1,0:T(8,128)(2,1)S(1)}, u32[]{:S(2)}) %copy-start) | copy-done | bytes 3932184
  17.5 0.0 copy-start.3
  17.5 0.0 copy-start.4
  17.5 11.6 %all-to-all-start = ((bf16[128,120,128]{2,1,0:T(8,128)(2,1)}), bf16[128,120,128]{2,1,0:T(8,128)(2,1)}, u32[]{:S(2)}, u32[]{:S(2)}) async-start(bf16[128,120,128]{2,1,0:T(8,128)(2,1)} %copy-done), calls=%async_computation | async-start | bytes 7864320 | tf_op jit(solution)/shard_map/all_to_all | solution.py:176
  29.1 48.8 %all-to-all-done = bf16[128,120,128]{2,1,0:T(8,128)(2,1)} async-done(((bf16[128,120,128]{2,1,0:T(8,128)(2,1)}), bf16[128,120,128]{2,1,0:T(8,128)(2,1)}, u32[]{:S(2)}, u32[]{:S(2)}) %all-to-all-start) | async-done | bytes 3932192 | tf_op jit(solution)/shard_map/all_to_all | solution.py:176
  77.9 0.0 copy-done.3
  77.9 0.0 copy-done.4
  77.9 9.6 %subspace_product.1 = f32[384,384]{1,0:T(8,128)S(1)} custom-call(s32[1]{0:T(128)} %bitcast.own_ref, bf16[16,8,120,128]{3,2,1,0:T(8,128)(2,1)} %bitcast.3.blocks_ref, bf16[2,384,384]{2,1,0:T(8,128)(2,1)S(1)} %copy-done.3, bf16[128,384]{1,0:T(8,128)(2,1)S(1)} %copy-done.4), custom_call_target="tpu_custom_call" | custom-call | tf_op jit(solution)/shard_map/subspace_product/pallas_call | solution.py:177
  87.5 14.9 %all_to_all.15 = f32[16,24,384]{2,1,0:T(8,128)S(1)} all-to-all(f32[16,24,384]{2,1,0:T(8,128)S(1)} %bitcast.8), channel_id=1, replica_groups=mesh['band'=16,'dom'=8] {'band'}, dimensions={0} | all-to-all | bytes 1179648 | tf_op jit(solution)/shard_map/all_to_all | solution.py:200
  102.4 12.6 %all_to_all.16 = f32[8,24,384]{2,1,0:T(8,128)S(1)} all-to-all(f32[8,24,384]{2,1,0:T(8,128)S(1)} %broadcast_in_dim.3), channel_id=1, replica_groups=mesh['band'=16,'dom'=8] {'dom'}, dimensions={0} | all-to-all | bytes 589824 | tf_op jit(solution)/shard_map/all_to_all | solution.py:202
  115.0 0.6 reduce_sum.19
  (3 shorter events, 0.1 us)
Async XLA Ops:
  0.7 1.5 %copy-start.1 = (bf16[24,6,6144]{2,0,1:T(8,128)(2,1)S(1)}, bf16[24,6,6144]{2,0,1:T(8,128)(2,1)}, u32[]{:S(2)}) copy-start(bf16[24,6,6144]{2,0,1:T(8,128)(2,1)} %param.5) | copy-start | bytes 5308420
  2.2 1.3 %copy-start.2 = (bf16[2,768,384]{2,1,0:T(8,128)(2,1)S(1)}, bf16[2,768,384]{2,1,0:T(8,128)(2,1)}, u32[]{:S(2)}) copy-start(bf16[2,768,384]{2,1,0:T(8,128)(2,1)} %constant.16.clone.plane_ref) | copy-start | bytes 3538948
  15.6 1.9 %copy-start = (bf16[128,120,128]{2,1,0:T(8,128)(2,1)}, bf16[128,120,128]{2,1,0:T(8,128)(2,1)S(1)}, u32[]{:S(2)}) copy-start(bf16[128,120,128]{2,1,0:T(8,128)(2,1)S(1)} %apply_upward.1) | copy-start | bytes 11796484
  17.5 60.4 %copy-start.3 = (bf16[2,384,384]{2,1,0:T(8,128)(2,1)S(1)}, bf16[2,384,384]{2,1,0:T(8,128)(2,1)}, u32[]{:S(2)}) copy-start(bf16[2,384,384]{2,1,0:T(8,128)(2,1)} %constant.17.clone.next_plane_ref) | copy-start | bytes 1769476
  17.5 60.4 %copy-start.4 = (bf16[128,384]{1,0:T(8,128)(2,1)S(1)}, bf16[128,384]{1,0:T(8,128)(2,1)}, u32[]{:S(2)}) copy-start(bf16[128,384]{1,0:T(8,128)(2,1)} %constant.18.clone.spread_ref) | copy-start | bytes 294916
  17.5 60.4 %all-to-all-start = ((bf16[128,120,128]{2,1,0:T(8,128)(2,1)}), bf16[128,120,128]{2,1,0:T(8,128)(2,1)}, u32[]{:S(2)}, u32[]{:S(2)}) async-start(bf16[128,120,128]{2,1,0:T(8,128)(2,1)} %copy-done), calls=%async_computation | async-start | bytes 7864320 | tf_op jit(solution)/shard_map/all_to_all | solution.py:176

commit v2 on v1

v2 whole, which is shorter than its diff:
```python
import functools
import math

import jax
import jax.numpy as jnp
import ml_dtypes
import numpy as np
from jax import lax
from jax.experimental import pallas as pl
from jax.experimental.pallas import tpu as pltpu
from jax.sharding import PartitionSpec as P

NZ = 64
LANES = 128
BLOCKS = 8
WIDTH = LANES // BLOCKS
FOLD = 16
REACH = 6


STENCIL = (
    -5369.0 / 1800.0,
    12.0 / 7.0,
    -15.0 / 56.0,
    10.0 / 189.0,
    -1.0 / 112.0,
    2.0 / 1925.0,
    -1.0 / 16632.0,
)


def halves(matrix):
    high = matrix.astype(ml_dtypes.bfloat16)
    low = (matrix - high.astype(np.float64)).astype(ml_dtypes.bfloat16)
    return high, low


def upward_plane():
    matrix = np.zeros((4 * LANES, LANES))
    out = np.arange(LANES)
    matrix[out, out] = -0.75 * STENCIL[0]
    for k in range(1, REACH + 1):
        matrix[out + k * NZ, out] += -0.5 * STENCIL[k]
        matrix[out // NZ * NZ + (out + k) % NZ, out] += -0.5 * STENCIL[k]
    return jnp.asarray(np.concatenate(halves(matrix), axis=1))


def upward_next(layers, rows):
    matrix = np.zeros((2 * LANES, 2 * LANES + 2 * WIDTH))
    for x in range(layers):
        for k in range(1, REACH + 1):
            there = x + k - layers
            for v in range(rows):
                start, end = (there * rows + v) * WIDTH, (x * rows + v) * WIDTH
                if 0 <= there < layers and start < 2 * LANES:
                    for j in range(WIDTH):
                        matrix[start + j, end + j] = -0.5 * STENCIL[k]
    high, low = halves(matrix)
    tail = np.zeros((2 * LANES, LANES - 4 * WIDTH), ml_dtypes.bfloat16)
    return jnp.asarray(np.concatenate([high[:, : 2 * LANES], low[:, : 2 * LANES], high[:, 2 * LANES :], low[:, 2 * LANES :], tail], axis=1))


def exchange_blocks(tiles):
    lane = lax.broadcasted_iota(jnp.int16, tiles[0].shape, 1)
    for bit in (4, 2, 1):
        upper = (lane & (bit * WIDTH)) != 0
        moved = list(tiles)
        for i in range(BLOCKS):
            if not i & bit:
                a, b = tiles[i], tiles[i | bit]
                moved[i] = jnp.where(upper, pltpu.roll(b, bit * WIDTH, 1), a)
                moved[i | bit] = jnp.where(upper, b, pltpu.roll(a, LANES - bit * WIDTH, 1))
        tiles = moved
    return tiles


def coded(potential_ref, rows):
    field = [potential_ref[x : x + 1, v * LANES : (v + 1) * LANES] for x in range(potential_ref.shape[0]) for v in range(rows)]
    field = jnp.concatenate(field + [jnp.zeros((3 * BLOCKS - len(field), LANES), jnp.float32)], axis=0)
    high = jnp.floor(field * 64.0 + 0.5) * (1.0 / 64.0)
    low = field - high
    pairs = jnp.floor(low[8:16] * 1024.0 + 0.5)
    pairs = 17.0 * pltpu.roll(pairs, 4, 0) + pairs
    row = lax.broadcasted_iota(jnp.int32, pairs.shape, 0)
    mixed = jnp.where(row < 2, high[16:], jnp.where(row < 4, pltpu.roll(low[16:], 2, 0), pairs))
    return [high[:8], high[8:16], low[:8], mixed]


def decoded(codes):
    row = lax.broadcasted_iota(jnp.int32, codes.shape, 0)
    block = lax.broadcasted_iota(jnp.int32, codes.shape, 1) >> 4
    parts = []
    for at in range(4):
        part = jnp.where(block == 4 + at, codes, 0.0)
        for shift in (4, 2, 1):
            part = part + pltpu.roll(part, shift * WIDTH, 1)
        parts.append(part)
    first, second, low, mixed = parts
    upper = jnp.floor(mixed * (1.0 / 17.0) + 0.5)
    pairs = jnp.where(row < 4, pltpu.roll(upper, 4, 0), mixed - 17.0 * upper)
    field = [first + low, second + pairs * (1.0 / 1024.0), mixed + pltpu.roll(mixed, 6, 0)]
    return jnp.concatenate([jnp.sum(jnp.where(block == row, part, 0.0), axis=0, keepdims=True) for part in field], axis=1)


def apply_kernel(layers, bands, rows, place_ref, here_ref, next_ref, plane_ref, potential_ref, out_ref):
    here = here_ref[...]
    size = here.shape[0]
    many = here.shape[1] // LANES
    both = jnp.concatenate([here, next_ref[...]], axis=1)
    stacked = jnp.concatenate([both[:, v * LANES : (v + 4) * LANES] for v in range(many)], axis=0)
    applied = jnp.dot(stacked, plane_ref[...], preferred_element_type=jnp.float32)
    applied = applied[:, :LANES] + applied[:, LANES:]
    codes = coded(potential_ref, rows)
    for start in range(0, many, rows):
        psi, half = [], []
        for v in range(start, start + rows):
            center = here[:, v * LANES : (v + 1) * LANES].astype(jnp.float32)
            psi.append([center[x * bands : (x + 1) * bands] for x in range(layers)])
            half.append([])
            for x in range(layers):
                total = applied[v * size + x * bands : v * size + (x + 1) * bands]
                for k in range(1, layers - x):
                    total = total + (-0.5 * STENCIL[k]) * psi[-1][x + k]
                half[-1].append(total)
        psi = [psi[v][x] for x in range(layers) for v in range(rows)]
        half = [half[v][x] for x in range(layers) for v in range(rows)]
        mine = pl.program_id(0) * (many // rows) + start // rows == place_ref[0]
        last = psi[16:] + half[16:]
        last = [part[:FOLD] for part in last] + [jnp.concatenate([part[FOLD:], jnp.where(mine, code, 0.0)], axis=0) for part, code in zip(last, codes)]
        tiles = [
            jnp.concatenate([psi[i], psi[8 + i], half[i], half[8 + i], last[i]], axis=0).astype(jnp.bfloat16)
            for i in range(BLOCKS)
        ]
        for there, tile in enumerate(exchange_blocks(tiles)):
            out_ref[there, start // rows] = tile


def product_kernel(bands, scaling, blocks_ref, next_plane_ref, out_ref, total, after, after_rest, rests):
    step = pl.program_id(0)
    count = blocks_ref.shape[1]
    size = count * bands

    def group(at):
        return blocks_ref[0, :, at * bands : (at + 1) * bands, :].reshape(size, LANES)

    psi = jnp.concatenate([group(0), group(1)], axis=1)
    rest = blocks_ref[0, :, 4 * bands :, :].astype(jnp.float32)
    codes = rest[:, bands - FOLD :]
    beside = pltpu.roll(rest, LANES // 2, 2)[:, : bands - FOLD]
    rest = jnp.concatenate([rest, beside], axis=1).reshape(size, LANES)

    @pl.when(step == 0)
    def _():
        total[...] = jnp.zeros_like(total)

    @pl.when(step > 0)
    def _():
        beyond = jnp.dot(after[...], next_plane_ref[...], preferred_element_type=jnp.float32)
        field = 0.5 * decoded(jnp.sum(codes, axis=0))
        half = jnp.concatenate([group(2), group(3)], axis=1).astype(jnp.float32)
        half = half + beyond[:, : 2 * LANES] + beyond[:, 2 * LANES : 4 * LANES]
        half = half + field[:, : 2 * LANES] * psi.astype(jnp.float32)
        total[...] += lax.dot_general(
            psi, half.astype(jnp.bfloat16), (((1,), (1,)), ((), ())), preferred_element_type=jnp.float32
        )
        beyond_rest = beyond[:, 4 * LANES :]
        beyond_rest = beyond_rest + pltpu.roll(beyond_rest + rest, LANES - 2 * WIDTH, 1)
        beyond_rest = beyond_rest + (-0.5 * STENCIL[REACH]) * after_rest[...] + field[:, 2 * LANES :] * rest
        rests[step - 1, 0] = rest
        rests[step - 1, 1] = beyond_rest

    after[...] = psi
    after_rest[...] = rest

    @pl.when(step == pl.num_programs(0) - 1)
    def _():
        lane = lax.broadcasted_iota(jnp.int32, rest.shape, 1)

        def gathered(which):
            parts = []
            for first in range(0, BLOCKS, 4):
                part = jnp.where(lane < 2 * WIDTH, rests[first, which], 0.0)
                for i in range(1, 4):
                    place = (lane >= 2 * WIDTH * i) & (lane < 2 * WIDTH * (i + 1))
                    part = jnp.where(place, pltpu.roll(rests[first + i, which], 2 * WIDTH * i, 1), part)
                parts.append(part)
            return jnp.concatenate(parts, axis=1).astype(jnp.bfloat16)

        whole = total[...] + lax.dot_general(
            gathered(0), gathered(1), (((1,), (1,)), ((), ())), preferred_element_type=jnp.float32
        )
        whole = whole * scaling
        out_ref[...] = whole + whole.T


def project(bands, scaling, rows, layers, received):
    doms, count, chunk, _ = received.shape
    size = count * bands
    return pl.pallas_call(
        functools.partial(product_kernel, bands, scaling),
        grid=(doms + 1,),
        in_specs=[
            pl.BlockSpec((1, count, chunk, LANES), lambda i: ((doms - i) % doms, 0, 0, 0)),
            pl.BlockSpec((2 * LANES, 5 * LANES), lambda i: (0, 0)),
        ],
        out_specs=pl.BlockSpec((size, size), lambda i: (0, 0)),
        out_shape=jax.ShapeDtypeStruct((size, size), jnp.float32),
        scratch_shapes=[
            pltpu.VMEM((size, size), jnp.float32),
            pltpu.VMEM((size, 2 * LANES), jnp.bfloat16),
            pltpu.VMEM((size, LANES), jnp.float32),
            pltpu.VMEM((doms, 2, size, LANES), jnp.float32),
        ],
        compiler_params=pltpu.CompilerParams(vmem_limit_bytes=24 * 2**20),
        name="subspace_product",
    )(received, pltpu.with_memory_space_constraint(upward_next(layers, rows), pltpu.HBM))


def per_device(orbitals, potential):
    bands, layers, cells_row = orbitals.shape
    count = lax.axis_size("band")
    doms = lax.axis_size("dom")
    cells = cells_row // count
    rows = cells // LANES
    chunk = 4 * bands + FOLD
    size = count * bands
    cells_all = layers * doms * cells_row
    group = 4
    place = lax.axis_index("band").astype(jnp.int32).reshape(1)
    planes = jnp.transpose(orbitals, (1, 0, 2)).reshape(layers * bands, cells_row)
    planes = pltpu.with_memory_space_constraint(planes, pltpu.HBM)
    packed = pl.pallas_call(
        functools.partial(apply_kernel, layers, bands, rows),
        grid=(count // group,),
        in_specs=[
            pl.BlockSpec(memory_space=pltpu.SMEM),
            pl.BlockSpec((layers * bands, group * cells), lambda i: (0, i)),
            pl.BlockSpec((layers * bands, cells), lambda i: (0, (i + 1) * group % count)),
            pl.BlockSpec((4 * LANES, 2 * LANES), lambda i: (0, 0)),
            pl.BlockSpec((layers, cells), lambda i: (0, 0)),
        ],
        out_specs=pl.BlockSpec((doms, group, chunk, LANES), lambda i: (0, i, 0, 0)),
        out_shape=jax.ShapeDtypeStruct((doms, count, chunk, LANES), jnp.bfloat16),
        compiler_params=pltpu.CompilerParams(vmem_limit_bytes=24 * 2**20),
        name="apply_upward",
    )(place, planes, planes, pltpu.with_memory_space_constraint(upward_plane(), pltpu.HBM), potential)
    received = lax.all_to_all(packed.reshape(doms * count, chunk, LANES), ("dom", "band"), 0, 0, tiled=True)
    partial = project(bands, 1.0 / math.sqrt(cells_all), rows, layers, received.reshape(doms, count, chunk, LANES))
    own_rows = lax.all_to_all(partial.reshape(count, bands, size), "band", 0, 0, tiled=True).sum(0)
    copies = jnp.broadcast_to(own_rows, (doms, bands, size))
    return lax.all_to_all(copies, "dom", 0, 0, tiled=True).sum(0)


def solution(mesh):
    placed = (P("band", "dom", None), P("dom", "band"))
    return jax.shard_map(
        per_device, mesh=mesh, in_specs=placed, out_specs=P("band", None), check_vma=False
    )
```

time: 116 us -> 101 us (0.87)
  blocking collectives: 27.4 us -> 85.1 us
  waiting for transfers between devices: 48.8 us -> 0 us
  starting transfers between devices: 11.6 us -> 0 us
  Pallas kernels: 21.7 us -> 13.8 us
  local copies, waits for them, and re-layouts: 5.39 us -> 0.73 us
    all_to_all x0 -> x1, blocking collectives: none -> 58.3 us  [per_device(): lax.all_to_all(packed.reshape(doms * count, chunk, LANES), ('dom', 'band'...]
    all_to_all x1 -> x0, waiting for transfers between devices: 48.8 us -> none  [per_device(): received = lax.all_to_all(packed, ('band', 'dom'), 0, 0, tiled=True)]
    all_to_all x1 -> x0, starting transfers between devices: 11.6 us -> none  [per_device(): received = lax.all_to_all(packed, ('band', 'dom'), 0, 0, tiled=True)]
    pallas_call x2, Pallas kernels: 21.7 us -> 13.8 us  [the longest x1 7.89 us: project(): pl.pallas_call(functools.partial(product_kernel, bands, scaling), grid=(d...]
    unnamed x10 -> x2, local copies, waits for them, and re-layouts: 4.65 us -> 0.71 us
  transfers between devices with their start and end apart: 1 -> 0, of which waited for: 1 -> 0; matrix products, arithmetic and copies ran while one was open for 0% -> 0% of each run, Pallas kernels for 0% -> 0%
where the time goes in v2:
time: 101 us; the launch traced here: 100 us
  blocking collectives  85.1 us (84%)
  Pallas kernels  13.8 us (14%)
    all_to_all x1, blocking collectives, per_device(): lax.all_to_all(packed.reshape(doms * count, chunk, LANES), ('dom', 'band'...  58.3 us
    all_to_all x1, blocking collectives, per_device(): lax.all_to_all(partial.reshape(count, bands, size), 'band', 0, 0, tiled=T...  14.2 us
    all_to_all x1, blocking collectives, per_device(): return lax.all_to_all(copies, 'dom', 0, 0, tiled=True).sum(0)  12.6 us
    pallas_call x1, Pallas kernels, project(): pl.pallas_call(functools.partial(product_kernel, bands, scaling), grid=(d...  7.89 us
    pallas_call x1, Pallas kernels, per_device(): pl.pallas_call(functools.partial(apply_kernel, layers, bands, rows), grid...  5.94 us

profile of v2, /device:TPU:0, one launch (start us, length us, event | category | flops | bytes accessed | tf_op | source)
XLA Modules:
  0.0 100.3 jit_solution(4158475889804259294)
XLA Ops:
  0.0 0.0 copy-start
  0.0 0.7 copy-done
  0.7 5.9 %apply_upward.1 = bf16[8,16,112,128]{3,2,1,0:T(8,128)(2,1)S(1)} custom-call(s32[1]{0:T(128)} %bitcast.place_ref, bf16[144,6144]{1,0:T(8,128)(2,1)} %bitcast.10, bf16[144,6144]{1,0:T(8,128)(2,1)} %bitcast.11, bf16[512,256]{1,0:T(8,128)(2,1)} %constant.12.clone.plane_ref, f32[6,384]{1,0:T(8,128)S(1)} %copy-done), custom_call_target="tpu_custom_call" | custom-call | tf_op jit(solution)/shard_map/apply_upward/pallas_call | solution.py:232
  6.7 58.3 %all_to_all.15 = bf16[128,112,128]{2,1,0:T(8,128)(2,1)S(1)} all-to-all(bf16[128,112,128]{2,1,0:T(8,128)(2,1)S(1)} %bitcast.7), channel_id=1, replica_groups=mesh['band'=16,'dom'=8] {'dom','band'}, dimensions={0} | all-to-all | bytes 7340032 | tf_op jit(solution)/shard_map/all_to_all | solution.py:247
  64.9 7.9 %subspace_product.1 = f32[384,384]{1,0:T(8,128)S(1)} custom-call(bf16[8,16,112,128]{3,2,1,0:T(8,128)(2,1)S(1)} %bitcast.8, bf16[256,640]{1,0:T(8,128)(2,1)} %constant.13.clone.next_plane_ref), custom_call_target="tpu_custom_call" | custom-call | tf_op jit(solution)/shard_map/subspace_product/pallas_call | solution.py:199
  72.8 14.2 %all_to_all.16 = f32[16,24,384]{2,1,0:T(8,128)S(1)} all-to-all(f32[16,24,384]{2,1,0:T(8,128)S(1)} %bitcast.9), channel_id=1, replica_groups=mesh['band'=16,'dom'=8] {'band'}, dimensions={0} | all-to-all | bytes 1179648 | tf_op jit(solution)/shard_map/all_to_all | solution.py:249
  87.0 12.6 %all_to_all.17 = f32[8,24,384]{2,1,0:T(8,128)S(1)} all-to-all(f32[8,24,384]{2,1,0:T(8,128)S(1)} %broadcast_in_dim.3), channel_id=1, replica_groups=mesh['band'=16,'dom'=8] {'dom'}, dimensions={0} | all-to-all | bytes 589824 | tf_op jit(solution)/shard_map/all_to_all | solution.py:251
  99.7 0.6 reduce_sum.19
  (2 shorter events, 0.1 us)
Async XLA Ops:
  0.0 0.7 copy-start

commit v3 on v0

v3 whole, which is shorter than its diff:
```python
import functools
import math

import jax
import jax.numpy as jnp
import ml_dtypes
import numpy as np
from jax import lax
from jax.experimental import pallas as pl
from jax.experimental.pallas import tpu as pltpu
from jax.sharding import PartitionSpec as P

NZ = 64
LANES = 128
BLOCKS = 8
WIDTH = 8
TALL = 6
REACH = 6
FOLD = 16
WINDOWS = ((-3, -2, -1, 0, 1, 2, 3), (-2, -1, 1, 2, 3, 4), (-1, 2, 3, 4, 5))


STENCIL = (
    -5369.0 / 1800.0,
    12.0 / 7.0,
    -15.0 / 56.0,
    10.0 / 189.0,
    -1.0 / 112.0,
    2.0 / 1925.0,
    -1.0 / 16632.0,
)


def halves(matrix):
    high = matrix.astype(ml_dtypes.bfloat16)
    low = (matrix - high.astype(np.float64)).astype(ml_dtypes.bfloat16)
    return high, low


def sent_plane():
    matrices = []
    for v, window in enumerate(WINDOWS):
        matrix = np.zeros((len(window) * LANES, LANES))
        for out in range(LANES):
            y, z = 2 * v + out // NZ, out % NZ
            for at, other in enumerate(window):
                for half in range(2):
                    there = 2 * other + half
                    k = abs(there - y)
                    if 1 <= k <= REACH and (there > y or there < 0):
                        matrix[at * LANES + half * NZ + z, out] += -0.5 * STENCIL[k]
            start = window.index(v) * LANES + out // NZ * NZ
            for k in range(1, REACH + 1):
                matrix[start + (z + k) % NZ, out] += -0.5 * STENCIL[k]
                if z % WIDTH - k < 0:
                    matrix[start + (z - k) % NZ, out] += -0.5 * STENCIL[k]
        matrices.append(matrix)
    return jnp.asarray(np.concatenate(halves(np.concatenate(matrices)), axis=1))


def placed(x, y, j):
    index = 3 * (x % 3) + y // 2
    half = y % 2 * NZ + j
    return (x // 3, half + index * WIDTH) if index < BLOCKS else (2, half + x // 3 * WIDTH)


def upward_next(layers):
    matrix = np.zeros((2 * LANES, 3 * LANES))
    for x in range(layers):
        for there in range(x + 1):
            for y in range(TALL):
                for j in range(WIDTH):
                    (group, lane), (group_in, lane_in) = placed(x, y, j), placed(there, y, j)
                    if group_in < 2:
                        matrix[group_in * LANES + lane_in, group * LANES + lane] = -0.5 * STENCIL[there + layers - x]
    rest = [np.roll(matrix[:, 2 * LANES :], 2 * WIDTH * i, axis=1) for i in range(4)]
    return tuple(
        jnp.asarray(np.concatenate(halves(each), axis=1)) for each in (matrix[:, : 2 * LANES], np.concatenate(rest))
    )


def upward_block():
    matrix = np.zeros((2 * LANES, LANES))
    rest = np.zeros((LANES, LANES))
    for x in range(3):
        for y in range(TALL):
            for j in range(WIDTH):
                ends = [(x + k, y, j, k) for k in range(1, 3 - x)]
                ends += [(x, y + k, j, k) for k in range(1, TALL - y)]
                ends += [(x, y, j + k, k) for k in range(1, min(REACH, WIDTH - 1 - j) + 1)]
                group, lane = placed(x, y, j)
                for x_in, y_in, j_in, k in ends:
                    group_in, lane_in = placed(x_in, y_in, j_in)
                    if group == 0:
                        matrix[group_in // 2 * LANES + lane_in, lane] = -0.5 * STENCIL[k]
                    else:
                        for block in range(BLOCKS):
                            rest[lane_in + block * WIDTH, lane + block * WIDTH] = -0.5 * STENCIL[k]
    layers = [np.concatenate([matrix[:LANES], np.roll(matrix[LANES:], 2 * WIDTH * i, axis=0)]) for i in range(4)]
    return tuple(jnp.asarray(np.concatenate(halves(each), axis=1)) for each in (np.concatenate(layers), rest))


def exchange_blocks(tiles):
    lane = lax.broadcasted_iota(jnp.int16, tiles[0].shape, 1)
    for bit in (4, 2, 1):
        upper = (lane & (bit * WIDTH)) != 0
        moved = list(tiles)
        for i in range(BLOCKS):
            if not i & bit:
                a, b = tiles[i], tiles[i | bit]
                moved[i] = jnp.where(upper, pltpu.roll(b, bit * WIDTH, 1), a)
                moved[i | bit] = jnp.where(upper, b, pltpu.roll(a, LANES - bit * WIDTH, 1))
        tiles = moved
    return tiles


def coded(potential_ref):
    order = [(x, v) for x in range(6) for v in range(3) if x % 3 + v < 4] + [(2, 2), (5, 2)]
    field = [potential_ref[x : x + 1, v * LANES : (v + 1) * LANES] for x, v in order]
    field = jnp.concatenate(field + [jnp.zeros((3 * BLOCKS - len(field), LANES), jnp.float32)], axis=0)
    pieces = []
    for _ in range(3):
        piece = field.astype(jnp.bfloat16).astype(jnp.float32)
        pieces.append(piece)
        field = field - piece
    high, middle, low = pieces
    mixed = high[16:] + pltpu.roll(middle[16:], 2, 0) + pltpu.roll(low[16:], 4, 0)
    return [high[:16], middle[:16], mixed, low[:8], low[8:16]]


def decoded(codes):
    doms, rows, _ = codes.shape
    codes = codes.reshape(doms * rows, LANES)
    block = (lax.broadcasted_iota(jnp.int32, codes.shape, 1) >> 3) & (BLOCKS - 1)

    def repeated(at):
        part = jnp.where(block == at, codes, 0.0)
        if at:
            part = pltpu.roll(part, LANES - at * WIDTH, 1)
        for shift in (1, 2, 4):
            part = part + pltpu.roll(part, shift * WIDTH, 1)
        return part.reshape(doms, rows, LANES)

    whole = repeated(3) + repeated(7)
    mixed = repeated(4)[:, 8:]
    mixed = mixed + pltpu.roll(mixed, 6, 1) + pltpu.roll(mixed, 4, 1)
    field = [whole[:, :8] + repeated(5)[:, 8:], whole[:, 8:] + repeated(6)[:, 8:], mixed]
    own = lax.broadcasted_iota(jnp.int32, mixed.shape, 1) == (lax.broadcasted_iota(jnp.int32, mixed.shape, 2) >> 3) & (BLOCKS - 1)
    return jnp.concatenate([jnp.sum(jnp.where(own, part, 0.0), axis=1, keepdims=True) for part in field], axis=2)


def apply_kernel(layers, bands, rows, place_ref, before_ref, here_ref, next_ref, plane_ref, potential_ref, out_ref):
    here = here_ref[...]
    size = here.shape[0]
    many = here.shape[1] // LANES
    around = jnp.concatenate([before_ref[...], here, next_ref[...]], axis=1)
    applied, start = [], 0
    for window in WINDOWS:
        stacked = jnp.concatenate(
            [
                jnp.concatenate([around[:, (rows + at + i) * LANES : (rows + at + i + 1) * LANES] for i in window], axis=1)
                for at in range(0, many, rows)
            ],
            axis=0,
        )
        end = start + len(window) * LANES
        part = jnp.dot(stacked, plane_ref[start:end], preferred_element_type=jnp.float32)
        applied.append(part[:, :LANES] + part[:, LANES:])
        start = end
    codes = coded(potential_ref)
    lane = lax.broadcasted_iota(jnp.int32, (bands, LANES), 1)
    for at in range(many // rows):
        psi = [[] for _ in range(layers)]
        sent = [[] for _ in range(layers // 2)]
        lower = ((lane >> 3) & 1) != at % 2
        for v in range(rows):
            center = here[:, (at * rows + v) * LANES : (at * rows + v + 1) * LANES].astype(jnp.float32)
            center = [center[x * bands : (x + 1) * bands] for x in range(layers)]
            total = []
            for x in range(layers):
                part = applied[v][at * size + x * bands : at * size + (x + 1) * bands]
                for other in range(layers):
                    if other > x or (x >= 3 and other < 3):
                        part = part + (-0.5 * STENCIL[abs(other - x)]) * center[other]
                total.append(part)
                psi[x].append(center[x])
            for x in range(layers // 2):
                sent[x].append(jnp.where(lower, total[x], total[x + 3]))
        low, high, sent = sum(psi[:3], []), sum(psi[3:], []), sum(sent, [])
        last = [low[8], high[8], sent[8]]
        last = [each[:FOLD] for each in last] + codes[:1] + [
            jnp.concatenate([each[FOLD:], beside], axis=0) for each, beside in zip(last, codes[2:])
        ] + codes[1:2]
        tiles = [jnp.concatenate([low[i], high[i], sent[i], last[i]], axis=0).astype(jnp.bfloat16) for i in range(BLOCKS)]
        for there, tile in enumerate(exchange_blocks(tiles)):
            out_ref[there, at] = tile


def product_kernel(bands, scaling, place_ref, blocks_ref, *refs):
    matrices, (out_ref, psi_ref, half_ref, psi_rest, sent_rest, field, field_rest), held, arrived = refs[:4], refs[4:11], refs[11:15], refs[15]
    copies = [pltpu.make_async_copy(matrices[i], held[i], arrived.at[i]) for i in range(4)]
    for copy in copies:
        copy.start()
    next_ref, next_rest_ref, block_ref, rest_ref = held
    doms, count = blocks_ref.shape[:2]
    size = count * bands
    even = place_ref[1] == 0
    block = (lax.broadcasted_iota(jnp.int32, (size, LANES), 1) >> 3) & (BLOCKS - 1)
    quads = doms // 4

    def pair(dom):
        return pl.ds(pl.multiple_of(dom * (2 * LANES), 2 * LANES), 2 * LANES)

    field[...] = 0.5 * decoded(blocks_ref[:, place_ref[0], 3 * bands :, :].astype(jnp.float32)) - 0.75 * STENCIL[0]

    @pl.loop(0, doms)
    def _(dom):
        quad, i = dom >> 2, dom & 3
        last = blocks_ref[dom, :, 3 * bands :, :].astype(jnp.float32)
        row = field[dom]
        beside = pltpu.roll(last[:, : bands - FOLD], LANES - 4 * WIDTH, 2)
        last = jnp.concatenate([last, beside], axis=1).reshape(size, LANES)
        mine = block >> 1 == i
        psi_rest[quad] = jnp.where(mine, pltpu.roll(last, 2 * WIDTH * i, 1), psi_rest[quad])
        sent_rest[quad] = jnp.where(mine, pltpu.roll(last, (2 * WIDTH * (i + 7)) & (LANES - 1), 1), sent_rest[quad])
        field_rest[quad] = jnp.where(mine[:1], pltpu.roll(row[:, 2 * LANES :], 2 * WIDTH * i, 1), field_rest[quad])
        psi_ref[:, pair(dom)] = jnp.concatenate(
            [blocks_ref[dom, :, at * bands : (at + 1) * bands, :].reshape(size, LANES) for at in range(2)], axis=1
        )

    for copy in copies:
        copy.wait()

    @pl.loop(0, doms)
    def _(dom):
        i, after = dom & 3, (dom + 1) & (doms - 1)
        psi = psi_ref[:, pair(dom)]
        low, high = psi[:, :LANES], psi[:, LANES:]
        beyond = jnp.dot(psi_ref[:, pair(after)], next_ref[...], preferred_element_type=jnp.float32)
        kept = psi_rest[dom >> 2]
        kept = jnp.where(even, kept, pltpu.roll(kept, LANES - WIDTH, 1)).astype(jnp.bfloat16)
        kept = jnp.concatenate([jnp.where(even, low, high), kept], axis=1)
        rows = pl.ds(pl.multiple_of(i * (2 * LANES), 2 * LANES), 2 * LANES)
        inner = jnp.dot(kept, block_ref[rows, :], preferred_element_type=jnp.float32)
        inner = inner[:, :LANES] + inner[:, LANES:]
        sent = blocks_ref[dom, :, 2 * bands : 3 * bands, :].reshape(size, LANES).astype(jnp.float32)
        lead = psi_rest[after >> 2]
        from_here = 2 * (after & 3)
        lead = pltpu.roll(lead, ((2 - from_here) * WIDTH) & (LANES - 1), 1) * jnp.where(
            block[:1] == 2, -0.5 * STENCIL[5], 0.0
        ) + pltpu.roll(lead, ((5 - from_here) * WIDTH) & (LANES - 1), 1) * jnp.where(block[:1] == 5, -0.5 * STENCIL[4], 0.0)
        row = field[dom]
        half_low = beyond[:, :LANES] + beyond[:, 2 * LANES : 3 * LANES] + jnp.where(even, inner, sent)
        half_low = half_low + row[:, :LANES] * low.astype(jnp.float32)
        half_high = beyond[:, LANES : 2 * LANES] + beyond[:, 3 * LANES :] + jnp.where(even, sent, inner)
        half_high = half_high + lead + row[:, LANES : 2 * LANES] * high.astype(jnp.float32)
        half_ref[:, pair(dom)] = jnp.concatenate([half_low, half_high], axis=1).astype(jnp.bfloat16)

    for quad in range(quads):
        here, other = psi_rest[quad], psi_rest[(quad + 1) % quads]
        beyond = [psi_ref[:, 2 * ((4 * quad + i + 1) % doms) * LANES :][:, : 2 * LANES] for i in range(4)]
        beyond = jnp.dot(jnp.concatenate(beyond, axis=1), next_rest_ref[...], preferred_element_type=jnp.float32)
        ends = here.astype(jnp.bfloat16)
        inner = jnp.dot(ends, rest_ref[...], preferred_element_type=jnp.float32)
        inner = inner[:, :LANES] + inner[:, LANES:]
        after = jnp.where(block >= 6, pltpu.roll(other, 6 * WIDTH, 1), pltpu.roll(here, LANES - 2 * WIDTH, 1))
        half = beyond[:, :LANES] + beyond[:, LANES:] + field_rest[quad] * here + (-0.5 * STENCIL[6]) * after
        half = half + pltpu.roll(after, WIDTH, 1) * jnp.where(block[:1] & 1 == 1, -0.5 * STENCIL[3], 0.0)
        sent = jnp.where(even, pltpu.roll(sent_rest[quad], WIDTH, 1), sent_rest[quad])
        half = half + jnp.where(block & 1 == jnp.where(even, 0, 1), inner, sent)
        place = slice((2 * doms + quad) * LANES, (2 * doms + quad + 1) * LANES)
        psi_ref[:, place] = ends
        half_ref[:, place] = half.astype(jnp.bfloat16)

    whole = lax.dot_general(
        psi_ref[...], half_ref[...], (((1,), (1,)), ((), ())), preferred_element_type=jnp.float32
    )
    whole = whole * scaling
    out_ref[...] = whole + whole.T


def project(bands, scaling, layers, place, received):
    doms, count, chunk, _ = received.shape
    size = count * bands
    width = (2 * doms + doms // 4) * LANES
    whole = pl.BlockSpec(memory_space=pltpu.VMEM)
    matrices = [*upward_next(layers), *upward_block()]
    return pl.pallas_call(
        functools.partial(product_kernel, bands, scaling),
        in_specs=[pl.BlockSpec(memory_space=pltpu.SMEM), whole] + [pl.BlockSpec(memory_space=pl.ANY)] * 4,
        out_specs=whole,
        out_shape=jax.ShapeDtypeStruct((size, size), jnp.float32),
        scratch_shapes=[
            pltpu.VMEM((size, width), jnp.bfloat16),
            pltpu.VMEM((size, width), jnp.bfloat16),
            pltpu.VMEM((doms // 4, size, LANES), jnp.float32),
            pltpu.VMEM((doms // 4, size, LANES), jnp.float32),
            pltpu.VMEM((doms, 1, 3 * LANES), jnp.float32),
            pltpu.VMEM((doms // 4, 1, LANES), jnp.float32),
            *[pltpu.VMEM(each.shape, each.dtype) for each in matrices],
            pltpu.SemaphoreType.DMA((4,)),
        ],
        compiler_params=pltpu.CompilerParams(vmem_limit_bytes=32 * 2**20),
        name="subspace_product",
    )(place, received, *[pltpu.with_memory_space_constraint(each, pltpu.HBM) for each in matrices])


def per_device(orbitals, potential):
    bands, layers, cells_row = orbitals.shape
    count = lax.axis_size("band")
    doms = lax.axis_size("dom")
    cells = cells_row // count
    rows = cells // LANES
    chunk = 3 * bands + FOLD
    size = count * bands
    cells_all = layers * doms * cells_row
    group = 4
    band, dom = lax.axis_index("band"), lax.axis_index("dom")
    place = jnp.stack([band, (band + dom) & 1]).astype(jnp.int32)
    planes = jnp.transpose(orbitals, (1, 0, 2)).reshape(layers * bands, cells_row)
    planes = pltpu.with_memory_space_constraint(planes, pltpu.HBM)
    packed = pl.pallas_call(
        functools.partial(apply_kernel, layers, bands, rows),
        grid=(count // group,),
        in_specs=[
            pl.BlockSpec(memory_space=pltpu.SMEM),
            pl.BlockSpec((layers * bands, cells), lambda i: (0, (i * group + count - 1) % count)),
            pl.BlockSpec((layers * bands, group * cells), lambda i: (0, i)),
            pl.BlockSpec((layers * bands, cells), lambda i: (0, (i + 1) * group % count)),
            pl.BlockSpec((18 * LANES, 2 * LANES), lambda i: (0, 0)),
            pl.BlockSpec((layers, cells), lambda i: (0, 0)),
        ],
        out_specs=pl.BlockSpec((doms, group, chunk, LANES), lambda i: (0, i, 0, 0)),
        out_shape=jax.ShapeDtypeStruct((doms, count, chunk, LANES), jnp.bfloat16),
        compiler_params=pltpu.CompilerParams(vmem_limit_bytes=24 * 2**20),
        name="apply_upward",
    )(
        place,
        planes,
        planes,
        planes,
        pltpu.with_memory_space_constraint(sent_plane(), pltpu.HBM),
        pltpu.with_memory_space_constraint(potential, pltpu.HBM),
    )
    received = lax.all_to_all(packed.reshape(doms * count, chunk, LANES), ("dom", "band"), 0, 0, tiled=True)
    partial = project(bands, 1.0 / math.sqrt(cells_all), layers, place, received.reshape(doms, count, chunk, LANES))
    own_rows = lax.all_to_all(partial.reshape(count, bands, size), "band", 0, 0, tiled=True).sum(0)
    copies = jnp.broadcast_to(own_rows, (doms, bands, size))
    return lax.all_to_all(copies, "dom", 0, 0, tiled=True).sum(0)


def solution(mesh):
    placed = (P("band", "dom", None), P("dom", "band"))
    return jax.shard_map(
        per_device, mesh=mesh, in_specs=placed, out_specs=P("band", None), check_vma=False
    )
```

time: 371 us -> 91.8 us (0.25)
  waiting for transfers between devices: 143 us -> 0 us
  local copies, waits for them, and re-layouts: 86.5 us -> 0.02 us
  other arithmetic: 43.8 us -> 0.75 us
  Pallas kernels: 0 us -> 14.2 us
  between operations: 13.5 us -> 0.03 us
  blocking collectives: 63.4 us -> 76.6 us
  matrix products: 12.8 us -> 0 us
  starting transfers between devices: 6.59 us -> 0 us
    all_gather x1 -> x0, waiting for transfers between devices: 143 us -> none  [per_device(): block_in = lax.all_gather(applied, 'band', axis=0, tiled=True)]
    slice x36 -> x0, local copies, waits for them, and re-layouts: 84.6 us -> none  [the longest x12 30.6 us: per_device(): jnp.roll(center, offset, 2)]
    all_to_all x0 -> x3, blocking collectives: none -> 76.6 us  [the longest x1 49.8 us: per_device(): lax.all_to_all(packed.reshape(doms * count, chunk, LANES), ('dom', 'band'...]
    psum x1 -> x0, blocking collectives: 42.5 us -> none  [per_device(): tile_rows = lax.psum(tile_rows, 'dom')]
    convert_element_type x1 -> x0, other arithmetic: 41.9 us -> none  [per_device(): applied = (-0.5 * laplace + field[None] * center).astype(jnp.bfloat16)]
    all_gather x1 -> x0, blocking collectives: 20.9 us -> none  [per_device(): field = lax.all_gather(potential, 'band', axis=1, tiled=True)]
    pallas_call x0 -> x2, Pallas kernels: none -> 14.2 us  [the longest x1 7.12 us: project(): pl.pallas_call(functools.partial(product_kernel, bands, scaling), in_spec...]
    dot_general x1 -> x0, matrix products: 12.8 us -> none  [contract(): lax.dot_general(left, right, (((1,), (1,)), ((), ())), preferred_element_...]
  transfers between devices with their start and end apart: 3 -> 0, of which waited for: 1 -> 0; matrix products, arithmetic and copies ran while one was open for 23% -> 0% of each run, Pallas kernels for 0% -> 0%
where the time goes in v3:
time: 91.8 us; the launch traced here: 91.6 us
  blocking collectives  76.6 us (83%)
  Pallas kernels  14.2 us (15%)
    all_to_all x1, blocking collectives, per_device(): lax.all_to_all(packed.reshape(doms * count, chunk, LANES), ('dom', 'band'...  49.8 us
    all_to_all x1, blocking collectives, per_device(): lax.all_to_all(partial.reshape(count, bands, size), 'band', 0, 0, tiled=T...  14.2 us
    all_to_all x1, blocking collectives, per_device(): return lax.all_to_all(copies, 'dom', 0, 0, tiled=True).sum(0)  12.6 us
    pallas_call x1, Pallas kernels, project(): pl.pallas_call(functools.partial(product_kernel, bands, scaling), in_spec...  7.12 us
    pallas_call x1, Pallas kernels, per_device(): pl.pallas_call(functools.partial(apply_kernel, layers, bands, rows), grid...  7.06 us

profile of v3, /device:TPU:0, one launch (start us, length us, event | category | flops | bytes accessed | tf_op | source)
XLA Modules:
  0.0 91.6 jit_solution(10531039919553646723)
XLA Ops:
  0.0 0.1 pad_add_fusion.place_ref
  0.1 7.1 %apply_upward.1 = bf16[8,16,88,128]{3,2,1,0:T(8,128)(2,1)S(1)} custom-call(s32[2]{0:T(128)S(1)} %pad_add_fusion.place_ref, bf16[144,6144]{1,0:T(8,128)(2,1)} %bitcast.11, bf16[144,6144]{1,0:T(8,128)(2,1)} %bitcast.12, bf16[144,6144]{1,0:T(8,128)(2,1)} %bitcast.13, bf16[2304,256]{1,0:T(8,128)(2,1)} %constant.23.clone.plane_ref, f32[6,384]{1,0:T(8,128)} %potential_ref.1), custom_call_target="tpu_custom_call" | custom-call | tf_op jit(solution)/shard_map/apply_upward/pallas_call | solution.py:322
  7.1 49.8 %all_to_all.15 = bf16[128,88,128]{2,1,0:T(8,128)(2,1)S(1)} all-to-all(bf16[128,88,128]{2,1,0:T(8,128)(2,1)S(1)} %bitcast.8), channel_id=1, replica_groups=mesh['band'=16,'dom'=8] {'dom','band'}, dimensions={0} | all-to-all | bytes 5767168 | tf_op jit(solution)/shard_map/all_to_all | solution.py:345
  56.9 7.1 %subspace_product.1 = f32[384,384]{1,0:T(8,128)S(1)} custom-call(s32[2]{0:T(128)S(1)} %pad_add_fusion.place_ref, bf16[8,16,88,128]{3,2,1,0:T(8,128)(2,1)S(1)} %bitcast.9, bf16[256,512]{1,0:T(8,128)(2,1)} %constant.24.clone.refs_0_, bf16[1024,256]{1,0:T(8,128)(2,1)} %constant.25.clone.refs_1_, bf16[1024,256]{1,0:T(8,128)(2,1)} %constant.26.clone.refs_2_, ...), custom_call_target="tpu_custom_call" | custom-call | tf_op jit(solution)/shard_map/subspace_product/pallas_call | solution.py:288
  64.1 14.2 %all_to_all.16 = f32[16,24,384]{2,1,0:T(8,128)S(1)} all-to-all(f32[16,24,384]{2,1,0:T(8,128)S(1)} %bitcast.10), channel_id=1, replica_groups=mesh['band'=16,'dom'=8] {'band'}, dimensions={0} | all-to-all | bytes 1179648 | tf_op jit(solution)/shard_map/all_to_all | solution.py:347
  78.3 12.6 %all_to_all.17 = f32[8,24,384]{2,1,0:T(8,128)S(1)} all-to-all(f32[8,24,384]{2,1,0:T(8,128)S(1)} %broadcast_in_dim.3), channel_id=1, replica_groups=mesh['band'=16,'dom'=8] {'dom'}, dimensions={0} | all-to-all | bytes 589824 | tf_op jit(solution)/shard_map/all_to_all | solution.py:349
  91.0 0.6 reduce_sum.19
  (2 shorter events, 0.1 us)

commit v4 on v3

--- a/solution.py
+++ b/solution.py
@@ -40,7 +40,7 @@
 def sent_plane():
     matrices = []
     for v, window in enumerate(WINDOWS):
-        matrix = np.zeros((len(window) * LANES, LANES))
+        matrix = np.zeros(((len(window) + 1) * LANES, LANES))
         for out in range(LANES):
             y, z = 2 * v + out // NZ, out % NZ
             for at, other in enumerate(window):
@@ -49,11 +49,11 @@
                     k = abs(there - y)
                     if 1 <= k <= REACH and (there > y or there < 0):
                         matrix[at * LANES + half * NZ + z, out] += -0.5 * STENCIL[k]
-            start = window.index(v) * LANES + out // NZ * NZ
+            own, beside = (at * LANES + out // NZ * NZ for at in (window.index(v), len(window)))
             for k in range(1, REACH + 1):
-                matrix[start + (z + k) % NZ, out] += -0.5 * STENCIL[k]
+                matrix[(own if z % WIDTH + k < WIDTH else beside) + (z + k) % NZ, out] += -0.5 * STENCIL[k]
                 if z % WIDTH - k < 0:
-                    matrix[start + (z - k) % NZ, out] += -0.5 * STENCIL[k]
+                    matrix[beside + (z - k) % NZ, out] += -0.5 * STENCIL[k]
         matrices.append(matrix)
     return jnp.asarray(np.concatenate(halves(np.concatenate(matrices)), axis=1))
 
@@ -149,55 +149,91 @@
     return jnp.concatenate([jnp.sum(jnp.where(own, part, 0.0), axis=1, keepdims=True) for part in field], axis=2)
 
 
-def apply_kernel(layers, bands, rows, place_ref, before_ref, here_ref, next_ref, plane_ref, potential_ref, out_ref):
-    here = here_ref[...]
-    size = here.shape[0]
-    many = here.shape[1] // LANES
-    around = jnp.concatenate([before_ref[...], here, next_ref[...]], axis=1)
-    applied, start = [], 0
-    for window in WINDOWS:
-        stacked = jnp.concatenate(
-            [
-                jnp.concatenate([around[:, (rows + at + i) * LANES : (rows + at + i + 1) * LANES] for i in window], axis=1)
-                for at in range(0, many, rows)
-            ],
-            axis=0,
-        )
-        end = start + len(window) * LANES
-        part = jnp.dot(stacked, plane_ref[start:end], preferred_element_type=jnp.float32)
-        applied.append(part[:, :LANES] + part[:, LANES:])
-        start = end
-    codes = coded(potential_ref)
-    lane = lax.broadcasted_iota(jnp.int32, (bands, LANES), 1)
-    for at in range(many // rows):
-        psi = [[] for _ in range(layers)]
-        sent = [[] for _ in range(layers // 2)]
-        lower = ((lane >> 3) & 1) != at % 2
-        for v in range(rows):
-            center = here[:, (at * rows + v) * LANES : (at * rows + v + 1) * LANES].astype(jnp.float32)
-            center = [center[x * bands : (x + 1) * bands] for x in range(layers)]
-            total = []
-            for x in range(layers):
-                part = applied[v][at * size + x * bands : at * size + (x + 1) * bands]
-                for other in range(layers):
-                    if other > x or (x >= 3 and other < 3):
-                        part = part + (-0.5 * STENCIL[abs(other - x)]) * center[other]
-                total.append(part)
-                psi[x].append(center[x])
-            for x in range(layers // 2):
-                sent[x].append(jnp.where(lower, total[x], total[x + 3]))
-        low, high, sent = sum(psi[:3], []), sum(psi[3:], []), sum(sent, [])
-        last = [low[8], high[8], sent[8]]
-        last = [each[:FOLD] for each in last] + codes[:1] + [
-            jnp.concatenate([each[FOLD:], beside], axis=0) for each, beside in zip(last, codes[2:])
-        ] + codes[1:2]
-        tiles = [jnp.concatenate([low[i], high[i], sent[i], last[i]], axis=0).astype(jnp.bfloat16) for i in range(BLOCKS)]
-        for there, tile in enumerate(exchange_blocks(tiles)):
-            out_ref[there, at] = tile
+def apply_kernel(layers, bands, rows, group, place_ref, planes_ref, plane_ref, potential_ref, out_ref, held, plane, potential, arrived):
+    size, width = planes_ref.shape
+    side, part = rows * LANES, width // 4
+    ends = [(width - side, 0, side)] + [(i * part, side + i * part, part) for i in range(4)] + [(0, side + width, side)]
+    copies = [
+        pltpu.make_async_copy(planes_ref.at[:, pl.ds(start, count)], held.at[:, pl.ds(end, count)], arrived.at[i])
+        for i, (start, end, count) in enumerate(ends)
+    ]
+    copies += [pltpu.make_async_copy(plane_ref, plane, arrived.at[6]), pltpu.make_async_copy(potential_ref, potential, arrived.at[7])]
+    for i in (7, 0, 1, 6, 2, 3, 4, 5):
+        copies[i].start()
+    for i in (7, 0, 1, 6):
+        copies[i].wait()
+    codes = coded(potential)
+    lane = lax.broadcasted_iota(jnp.int32, (BLOCKS, LANES), 1)
+    steps = width // (group * side)
+
+    @pl.loop(0, steps)
+    def _(step):
+        for i in range(2, 6):
+
+            @pl.when(step == (i - 1) * steps // 4 - 1)
+            def _():
+                copies[i].wait()
+
+        around = held[:, pl.ds(pl.multiple_of(step * (group * side), side), (group + 2) * side)]
+        low, high, even, odd = [], [], [], []
+        blank = jnp.zeros((-3 * bands % 16, LANES), jnp.float32)
+        lower = (lane[:1] >> 3) & 1 == 0
+        for v in range((group + 2) * rows):
+            center = around[:, v * LANES : (v + 1) * LANES].astype(jnp.float32)
+            low.append(center[: 3 * bands])
+            high.append(center[3 * bands :])
+            odd.append(jnp.where(lower, low[v], high[v]))
+            even.append(jnp.where(lower, high[v], low[v]))
+        layered = [even, odd]
+        spaced = [[jnp.concatenate([each, blank], axis=0).astype(jnp.bfloat16) for each in which] for which in layered]
+        applied, start = [], 0
+        for v, window in enumerate(WINDOWS):
+            stacked = jnp.concatenate(
+                [
+                    jnp.concatenate(
+                        [spaced[at % 2][rows * (at + 1) + i] for i in window] + [spaced[1 - at % 2][rows * (at + 1) + v]], axis=1
+                    )
+                    for at in range(group)
+                ],
+                axis=0,
+            )
+            end = start + (len(window) + 1) * LANES
+            applied.append(jnp.dot(stacked, plane[start:end], preferred_element_type=jnp.float32))
+            start = end
+        taller = spaced[0][0].shape[0]
+        weight = {k: -0.5 * STENCIL[k] for k in range(1, 4)}
+        for at in range(group):
+            mine, others = layered[at % 2], layered[1 - at % 2]
+            first = lower if at % 2 else ~lower
+            across = {i: jnp.where(first, -0.5 * STENCIL[3 + i], -0.5 * STENCIL[3 - i]) for i in range(-2, 3)}
+            sent = [[], [], []]
+            psi = [[] for _ in range(layers)]
+            for v in range(rows):
+                place = rows * (at + 1) + v
+                for x in range(3):
+                    slices = [slice(other * bands, (other + 1) * bands) for other in range(3)]
+                    total = applied[v][at * taller :][slices[x]]
+                    total = total[:, :LANES] + total[:, LANES:]
+                    for other in range(3):
+                        if other > x:
+                            total = total + weight[other - x] * mine[place][slices[other]]
+                        total = total + across[other - x] * others[place][slices[other]]
+                    sent[x].append(total)
+                    psi[x].append(low[place][slices[x]])
+                    psi[x + 3].append(high[place][slices[x]])
+            first, second, sent = sum(psi[:3], []), sum(psi[3:], []), sum(sent, [])
+            last = [first[8], second[8], sent[8]]
+            last = [each[:FOLD] for each in last] + codes[:1] + [
+                jnp.concatenate([each[FOLD:], beside], axis=0) for each, beside in zip(last, codes[2:])
+            ] + codes[1:2]
+            tiles = [jnp.concatenate([first[i], second[i], sent[i], last[i]], axis=0).astype(jnp.bfloat16) for i in range(BLOCKS)]
+            for there, tile in enumerate(exchange_blocks(tiles)):
+                out_ref[there, step * group + at] = tile
 
 
 def product_kernel(bands, scaling, place_ref, blocks_ref, *refs):
-    matrices, (out_ref, psi_ref, half_ref, psi_rest, sent_rest, field, field_rest), held, arrived = refs[:4], refs[4:11], refs[11:15], refs[15]
+    matrices, (kept_ref, given_ref, out_ref, psi_ref, half_ref, psi_rest, sent_rest, field, field_rest) = refs[:4], refs[4:13]
+    held, arrived = refs[13:17], refs[17]
     copies = [pltpu.make_async_copy(matrices[i], held[i], arrived.at[i]) for i in range(4)]
     for copy in copies:
         copy.start()
@@ -213,7 +249,7 @@
 
     field[...] = 0.5 * decoded(blocks_ref[:, place_ref[0], 3 * bands :, :].astype(jnp.float32)) - 0.75 * STENCIL[0]
 
-    @pl.loop(0, doms)
+    @pl.loop(0, doms, unroll=2)
     def _(dom):
         quad, i = dom >> 2, dom & 3
         last = blocks_ref[dom, :, 3 * bands :, :].astype(jnp.float32)
@@ -231,7 +267,7 @@
     for copy in copies:
         copy.wait()
 
-    @pl.loop(0, doms)
+    @pl.loop(0, doms, unroll=2)
     def _(dom):
         i, after = dom & 3, (dom + 1) & (doms - 1)
         psi = psi_ref[:, pair(dom)]
@@ -276,7 +312,15 @@
         psi_ref[...], half_ref[...], (((1,), (1,)), ((), ())), preferred_element_type=jnp.float32
     )
     whole = whole * scaling
-    out_ref[...] = whole + whole.T
+    whole = whole + whole.T
+    core = place_ref[0] & 1
+    for pair in range(count // 2):
+        for which in range(2):
+            rows = whole[(2 * pair + which) * bands : (2 * pair + which + 1) * bands]
+            out_ref[which, pair] = rows
+    first, second = out_ref[0], out_ref[1]
+    kept_ref[...] = jnp.where(core == 0, first, second)
+    given_ref[...] = jnp.where(core == 0, second, first)
 
 
 def project(bands, scaling, layers, place, received):
@@ -288,9 +332,10 @@
     return pl.pallas_call(
         functools.partial(product_kernel, bands, scaling),
         in_specs=[pl.BlockSpec(memory_space=pltpu.SMEM), whole] + [pl.BlockSpec(memory_space=pl.ANY)] * 4,
-        out_specs=whole,
-        out_shape=jax.ShapeDtypeStruct((size, size), jnp.float32),
+        out_specs=[whole] * 2,
+        out_shape=[jax.ShapeDtypeStruct((count // 2, bands, size), jnp.float32)] * 2,
         scratch_shapes=[
+            pltpu.VMEM((2, count // 2, bands, size), jnp.float32),
             pltpu.VMEM((size, width), jnp.bfloat16),
             pltpu.VMEM((size, width), jnp.bfloat16),
             pltpu.VMEM((doms // 4, size, LANES), jnp.float32),
@@ -305,46 +350,46 @@
     )(place, received, *[pltpu.with_memory_space_constraint(each, pltpu.HBM) for each in matrices])
 
 
+def pack(doms, count, place, orbitals, potential):
+    bands, layers, cells_row = orbitals.shape
+    cells = cells_row // count
+    rows = cells // LANES
+    chunk = 3 * bands + FOLD
+    group = 4
+    planes = jnp.transpose(orbitals, (1, 0, 2)).reshape(layers * bands, cells_row)
+    operands = [pltpu.with_memory_space_constraint(each, pltpu.HBM) for each in (planes, sent_plane(), potential)]
+    return pl.pallas_call(
+        functools.partial(apply_kernel, layers, bands, rows, group),
+        in_specs=[pl.BlockSpec(memory_space=pltpu.SMEM)] + [pl.BlockSpec(memory_space=pl.ANY)] * 3,
+        out_specs=pl.BlockSpec(memory_space=pltpu.VMEM),
+        out_shape=jax.ShapeDtypeStruct((doms, count, chunk, LANES), jnp.bfloat16),
+        scratch_shapes=[
+            pltpu.VMEM((layers * bands, cells_row + 2 * cells), jnp.bfloat16),
+            pltpu.VMEM((21 * LANES, 2 * LANES), jnp.bfloat16),
+            pltpu.VMEM(potential.shape, jnp.float32),
+            pltpu.SemaphoreType.DMA((8,)),
+        ],
+        compiler_params=pltpu.CompilerParams(vmem_limit_bytes=24 * 2**20),
+        name="apply_upward",
+    )(place, *operands)
+
+
 def per_device(orbitals, potential):
     bands, layers, cells_row = orbitals.shape
     count = lax.axis_size("band")
     doms = lax.axis_size("dom")
-    cells = cells_row // count
-    rows = cells // LANES
-    chunk = 3 * bands + FOLD
     size = count * bands
     cells_all = layers * doms * cells_row
-    group = 4
     band, dom = lax.axis_index("band"), lax.axis_index("dom")
     place = jnp.stack([band, (band + dom) & 1]).astype(jnp.int32)
-    planes = jnp.transpose(orbitals, (1, 0, 2)).reshape(layers * bands, cells_row)
-    planes = pltpu.with_memory_space_constraint(planes, pltpu.HBM)
-    packed = pl.pallas_call(
-        functools.partial(apply_kernel, layers, bands, rows),
-        grid=(count // group,),
-        in_specs=[
-            pl.BlockSpec(memory_space=pltpu.SMEM),
-            pl.BlockSpec((layers * bands, cells), lambda i: (0, (i * group + count - 1) % count)),
-            pl.BlockSpec((layers * bands, group * cells), lambda i: (0, i)),
-            pl.BlockSpec((layers * bands, cells), lambda i: (0, (i + 1) * group % count)),
-            pl.BlockSpec((18 * LANES, 2 * LANES), lambda i: (0, 0)),
-            pl.BlockSpec((layers, cells), lambda i: (0, 0)),
-        ],
-        out_specs=pl.BlockSpec((doms, group, chunk, LANES), lambda i: (0, i, 0, 0)),
-        out_shape=jax.ShapeDtypeStruct((doms, count, chunk, LANES), jnp.bfloat16),
-        compiler_params=pltpu.CompilerParams(vmem_limit_bytes=24 * 2**20),
-        name="apply_upward",
-    )(
-        place,
-        planes,
-        planes,
-        planes,
-        pltpu.with_memory_space_constraint(sent_plane(), pltpu.HBM),
-        pltpu.with_memory_space_constraint(potential, pltpu.HBM),
-    )
+    packed = pack(doms, count, place, orbitals, potential)
+    chunk = packed.shape[2]
     received = lax.all_to_all(packed.reshape(doms * count, chunk, LANES), ("dom", "band"), 0, 0, tiled=True)
-    partial = project(bands, 1.0 / math.sqrt(cells_all), layers, place, received.reshape(doms, count, chunk, LANES))
-    own_rows = lax.all_to_all(partial.reshape(count, bands, size), "band", 0, 0, tiled=True).sum(0)
+    kept, given = project(bands, 1.0 / math.sqrt(cells_all), layers, place, received.reshape(doms, count, chunk, LANES))
+    cores = [(i, i ^ 1) for i in range(count)]
+    same_core = [list(range(core, count, 2)) for core in range(2)]
+    kept = kept + lax.ppermute(given, "band", cores)
+    own_rows = lax.all_to_all(kept, "band", 0, 0, axis_index_groups=same_core, tiled=True).sum(0)
     copies = jnp.broadcast_to(own_rows, (doms, bands, size))
     return lax.all_to_all(copies, "dom", 0, 0, tiled=True).sum(0)
 

time: 91.8 us -> 88 us (0.959)
  blocking collectives: 76.6 us -> 72.6 us
  waiting for transfers between devices: 0 us -> 1.57 us
  Pallas kernels: 14.2 us -> 12.7 us
    all_to_all x1, blocking collectives: 14.2 us -> 10.8 us  [per_device(): lax.all_to_all(kept, 'band', 0, 0, axis_index_groups=same_core, tiled=True)]
    ppermute x0 -> x1, waiting for transfers between devices: none -> 1.57 us  [per_device(): kept = kept + lax.ppermute(given, 'band', cores)]
    pallas_call x1, Pallas kernels: 7.12 us -> 5.91 us  [project(): pl.pallas_call(functools.partial(product_kernel, bands, scaling), in_spec...]
  transfers between devices with their start and end apart: 0 -> 1, of which waited for: 0 -> 1; matrix products, arithmetic and copies ran while one was open for 0% -> 0% of each run, Pallas kernels for 0% -> 0%
where the time goes in v4:
time: 88 us; the launch traced here: 87.7 us
  blocking collectives  72.6 us (82%)
  Pallas kernels  12.7 us (14%)
  waiting for transfers between devices  1.57 us (2%)
    all_to_all x1, blocking collectives, per_device(): lax.all_to_all(packed.reshape(doms * count, chunk, LANES), ('dom', 'band'...  49.8 us
    all_to_all x1, blocking collectives, per_device(): return lax.all_to_all(copies, 'dom', 0, 0, tiled=True).sum(0)  12 us
    all_to_all x1, blocking collectives, per_device(): lax.all_to_all(kept, 'band', 0, 0, axis_index_groups=same_core, tiled=True)  10.8 us
    pallas_call x1, Pallas kernels, pack(): pl.pallas_call(functools.partial(apply_kernel, layers, bands, rows, group...  6.74 us
    pallas_call x1, Pallas kernels, project(): pl.pallas_call(functools.partial(product_kernel, bands, scaling), in_spec...  5.91 us
  transfers between devices with their start and end apart: 1, of which 1 were waited for; matrix products, arithmetic and copies ran while one was open for 0% of the time, Pallas kernels for 0%

profile of v4, /device:TPU:0, one launch (start us, length us, event | category | flops | bytes accessed | tf_op | source)
XLA Modules:
  0.0 87.7 jit_solution(13514803517079396845)
XLA Ops:
  0.0 0.1 pad_add_fusion.place_ref
  0.1 6.7 %apply_upward.1 = bf16[8,16,88,128]{3,2,1,0:T(8,128)(2,1)S(1)} custom-call(s32[2]{0:T(128)S(1)} %pad_add_fusion.place_ref, bf16[144,6144]{1,0:T(8,128)(2,1)} %bitcast.9, bf16[2688,256]{1,0:T(8,128)(2,1)} %constant.23.clone.plane_ref, f32[6,384]{1,0:T(8,128)} %potential_ref.1), custom_call_target="tpu_custom_call" | custom-call | tf_op jit(solution)/shard_map/apply_upward/pallas_call | solution.py:361
  6.8 49.8 %all_to_all.15 = bf16[128,88,128]{2,1,0:T(8,128)(2,1)S(1)} all-to-all(bf16[128,88,128]{2,1,0:T(8,128)(2,1)S(1)} %bitcast.8), channel_id=1, replica_groups=mesh['band'=16,'dom'=8] {'dom','band'}, dimensions={0} | all-to-all | bytes 5767168 | tf_op jit(solution)/shard_map/all_to_all | solution.py:387
  56.6 5.9 %subspace_product.1 = (f32[8,24,384]{2,1,0:T(8,128)S(1)}, f32[8,24,384]{2,1,0:T(8,128)S(1)}) custom-call(s32[2]{0:T(128)S(1)} %pad_add_fusion.place_ref, bf16[8,16,88,128]{3,2,1,0:T(8,128)(2,1)S(1)} %bitcast.7, bf16[256,512]{1,0:T(8,128)(2,1)} %constant.24.clone.refs_0_, bf16[1024,256]{1,0:T(8,128)(2,1)} %constant.25.clone.refs_1_, ...), custom_call_target="tpu_custom_call" | custom-call | tf_op jit(solution)/shard_map/subspace_product/pallas_call | solution.py:332
  62.5 0.1 collective-permute-start
  62.6 1.6 %collective-permute-done = f32[8,24,384]{2,1,0:T(8,128)S(1)} collective-permute-done((f32[8,24,384]{2,1,0:T(8,128)S(1)}, f32[8,24,384]{2,1,0:T(8,128)S(1)}, u32[]{:S(2)}, u32[]{:S(2)}) %collective-permute-start) | collective-permute-done | bytes 294944 | tf_op jit(solution)/shard_map/ppermute | solution.py:391
  64.2 10.8 %all_to_all.16 = f32[8,24,384]{2,1,0:T(8,128)S(1)} all-to-all(f32[8,24,384]{2,1,0:T(8,128)S(1)} %add.7), channel_id=1, replica_groups={{0,16,32,48,64,80,96,112},{8,24,40,56,72,88,104,120},{1,17,33,49,65,81,..., dimensions={0} | all-to-all | bytes 589824 | tf_op jit(solution)/shard_map/all_to_all | solution.py:392
  75.1 12.0 %all_to_all.17 = f32[8,24,384]{2,1,0:T(8,128)S(1)} all-to-all(f32[8,24,384]{2,1,0:T(8,128)S(1)} %broadcast_in_dim.3), channel_id=1, replica_groups=mesh['band'=16,'dom'=8] {'dom'}, dimensions={0} | all-to-all | bytes 589824 | tf_op jit(solution)/shard_map/all_to_all | solution.py:394
  87.1 0.6 reduce_sum.19
  (3 shorter events, 0.1 us)
Async XLA Ops:
  62.5 1.7 %collective-permute-start = (f32[8,24,384]{2,1,0:T(8,128)S(1)}, f32[8,24,384]{2,1,0:T(8,128)S(1)}, u32[]{:S(2)}, u32[]{:S(2)}) collective-permute-start(f32[8,24,384]{2,1,0:T(8,128)S(1)} %get-tuple-element.8), channel_id=1, source_target_pairs={{0,8},{8,0},{16,24},{24,16},{32,40},{40,32},{48,56},{56,48},{64,72... | collective-permute-start | bytes 884744 | tf_op jit(solution)/shard_map/ppermute | solution.py:391

commit v5 on v4

--- a/solution.py
+++ b/solution.py
@@ -75,7 +75,7 @@
                         matrix[group_in * LANES + lane_in, group * LANES + lane] = -0.5 * STENCIL[there + layers - x]
     rest = [np.roll(matrix[:, 2 * LANES :], 2 * WIDTH * i, axis=1) for i in range(4)]
     return tuple(
-        jnp.asarray(np.concatenate(halves(each), axis=1)) for each in (matrix[:, : 2 * LANES], np.concatenate(rest))
+        turned(np.concatenate(halves(each), axis=1)) for each in (matrix[:, : 2 * LANES], np.concatenate(rest))
     )
 
 
@@ -97,21 +97,22 @@
                         for block in range(BLOCKS):
                             rest[lane_in + block * WIDTH, lane + block * WIDTH] = -0.5 * STENCIL[k]
     layers = [np.concatenate([matrix[:LANES], np.roll(matrix[LANES:], 2 * WIDTH * i, axis=0)]) for i in range(4)]
-    return tuple(jnp.asarray(np.concatenate(halves(each), axis=1)) for each in (np.concatenate(layers), rest))
+    return tuple(turned(np.concatenate(halves(each), axis=1)) for each in (np.concatenate(layers), rest))
 
 
 def exchange_blocks(tiles):
     lane = lax.broadcasted_iota(jnp.int16, tiles[0].shape, 1)
-    for bit in (4, 2, 1):
+    tiles = [pltpu.roll(tile, i * WIDTH, 1) if i else tile for i, tile in enumerate(tiles)]
+    for bit in (1, 2, 4):
         upper = (lane & (bit * WIDTH)) != 0
-        moved = list(tiles)
-        for i in range(BLOCKS):
-            if not i & bit:
-                a, b = tiles[i], tiles[i | bit]
-                moved[i] = jnp.where(upper, pltpu.roll(b, bit * WIDTH, 1), a)
-                moved[i | bit] = jnp.where(upper, b, pltpu.roll(a, LANES - bit * WIDTH, 1))
-        tiles = moved
-    return tiles
+        tiles = [jnp.where(upper, tiles[(i + bit) % BLOCKS], tiles[i]) for i in range(BLOCKS)]
+    return [tiles[-c % BLOCKS] for c in range(BLOCKS)]
+
+
+def turned(matrix):
+    rows, columns = matrix.shape
+    tiles = matrix.reshape(rows // LANES, LANES, columns // LANES, LANES)
+    return jnp.asarray(np.stack([np.roll(tiles, (c * WIDTH, c * WIDTH), (1, 3)).reshape(rows, columns) for c in range(BLOCKS)]))
 
 
 def coded(potential_ref):
@@ -128,10 +129,10 @@
     return [high[:16], middle[:16], mixed, low[:8], low[8:16]]
 
 
-def decoded(codes):
+def decoded(codes, block):
     doms, rows, _ = codes.shape
     codes = codes.reshape(doms * rows, LANES)
-    block = (lax.broadcasted_iota(jnp.int32, codes.shape, 1) >> 3) & (BLOCKS - 1)
+    block = block[: doms * rows]
 
     def repeated(at):
         part = jnp.where(block == at, codes, 0.0)
@@ -145,11 +146,11 @@
     mixed = repeated(4)[:, 8:]
     mixed = mixed + pltpu.roll(mixed, 6, 1) + pltpu.roll(mixed, 4, 1)
     field = [whole[:, :8] + repeated(5)[:, 8:], whole[:, 8:] + repeated(6)[:, 8:], mixed]
-    own = lax.broadcasted_iota(jnp.int32, mixed.shape, 1) == (lax.broadcasted_iota(jnp.int32, mixed.shape, 2) >> 3) & (BLOCKS - 1)
+    own = lax.broadcasted_iota(jnp.int32, mixed.shape, 1) == block[: doms * BLOCKS].reshape(mixed.shape)
     return jnp.concatenate([jnp.sum(jnp.where(own, part, 0.0), axis=1, keepdims=True) for part in field], axis=2)
 
 
-def apply_kernel(layers, bands, rows, group, place_ref, planes_ref, plane_ref, potential_ref, out_ref, held, plane, potential, arrived):
+def apply_kernel(layers, bands, rows, group, place_ref, planes_ref, plane_ref, potential_ref, out_ref, held, plane, potential, spaced, arrived):
     size, width = planes_ref.shape
     side, part = rows * LANES, width // 4
     ends = [(width - side, 0, side)] + [(i * part, side + i * part, part) for i in range(4)] + [(0, side + width, side)]
@@ -174,24 +175,27 @@
             def _():
                 copies[i].wait()
 
-        around = held[:, pl.ds(pl.multiple_of(step * (group * side), side), (group + 2) * side)]
-        low, high, even, odd = [], [], [], []
+        base = step * (group * side)
         blank = jnp.zeros((-3 * bands % 16, LANES), jnp.float32)
         lower = (lane[:1] >> 3) & 1 == 0
+
+        def layered(v):
+            center = held[:, pl.ds(pl.multiple_of(base + v * LANES, LANES), LANES)].astype(jnp.float32)
+            return center[: 3 * bands], center[3 * bands :]
+
         for v in range((group + 2) * rows):
-            center = around[:, v * LANES : (v + 1) * LANES].astype(jnp.float32)
-            low.append(center[: 3 * bands])
-            high.append(center[3 * bands :])
-            odd.append(jnp.where(lower, low[v], high[v]))
-            even.append(jnp.where(lower, high[v], low[v]))
-        layered = [even, odd]
-        spaced = [[jnp.concatenate([each, blank], axis=0).astype(jnp.bfloat16) for each in which] for which in layered]
+            low, high = layered(v)
+            for which, upper in ((0, low), (1, high)):
+                each = jnp.where(lower, high if which == 0 else low, upper)
+                spaced[which, :, v * LANES : (v + 1) * LANES] = jnp.concatenate([each, blank], axis=0).astype(jnp.bfloat16)
         applied, start = [], 0
         for v, window in enumerate(WINDOWS):
             stacked = jnp.concatenate(
                 [
                     jnp.concatenate(
-                        [spaced[at % 2][rows * (at + 1) + i] for i in window] + [spaced[1 - at % 2][rows * (at + 1) + v]], axis=1
+                        [spaced[at % 2, :, (rows * (at + 1) + i) * LANES : (rows * (at + 1) + i + 1) * LANES] for i in window]
+                        + [spaced[1 - at % 2, :, (rows * (at + 1) + v) * LANES : (rows * (at + 1) + v + 1) * LANES]],
+                        axis=1,
                     )
                     for at in range(group)
                 ],
@@ -200,33 +204,35 @@
             end = start + (len(window) + 1) * LANES
             applied.append(jnp.dot(stacked, plane[start:end], preferred_element_type=jnp.float32))
             start = end
-        taller = spaced[0][0].shape[0]
+        taller = spaced.shape[1]
         weight = {k: -0.5 * STENCIL[k] for k in range(1, 4)}
         for at in range(group):
-            mine, others = layered[at % 2], layered[1 - at % 2]
             first = lower if at % 2 else ~lower
             across = {i: jnp.where(first, -0.5 * STENCIL[3 + i], -0.5 * STENCIL[3 - i]) for i in range(-2, 3)}
             sent = [[], [], []]
             psi = [[] for _ in range(layers)]
             for v in range(rows):
                 place = rows * (at + 1) + v
+                low, high = layered(place)
+                mine = jnp.where(first, low, high)
+                others = jnp.where(first, high, low)
                 for x in range(3):
                     slices = [slice(other * bands, (other + 1) * bands) for other in range(3)]
                     total = applied[v][at * taller :][slices[x]]
                     total = total[:, :LANES] + total[:, LANES:]
                     for other in range(3):
                         if other > x:
-                            total = total + weight[other - x] * mine[place][slices[other]]
-                        total = total + across[other - x] * others[place][slices[other]]
+                            total = total + weight[other - x] * mine[slices[other]]
+                        total = total + across[other - x] * others[slices[other]]
                     sent[x].append(total)
-                    psi[x].append(low[place][slices[x]])
-                    psi[x + 3].append(high[place][slices[x]])
-            first, second, sent = sum(psi[:3], []), sum(psi[3:], []), sum(sent, [])
-            last = [first[8], second[8], sent[8]]
+                    psi[x].append(low[slices[x]])
+                    psi[x + 3].append(high[slices[x]])
+            low, high, sent = sum(psi[:3], []), sum(psi[3:], []), sum(sent, [])
+            last = [low[8], high[8], sent[8]]
             last = [each[:FOLD] for each in last] + codes[:1] + [
                 jnp.concatenate([each[FOLD:], beside], axis=0) for each, beside in zip(last, codes[2:])
             ] + codes[1:2]
-            tiles = [jnp.concatenate([first[i], second[i], sent[i], last[i]], axis=0).astype(jnp.bfloat16) for i in range(BLOCKS)]
+            tiles = [jnp.concatenate([low[i], high[i], sent[i], last[i]], axis=0).astype(jnp.bfloat16) for i in range(BLOCKS)]
             for there, tile in enumerate(exchange_blocks(tiles)):
                 out_ref[there, step * group + at] = tile
 
@@ -234,20 +240,20 @@
 def product_kernel(bands, scaling, place_ref, blocks_ref, *refs):
     matrices, (kept_ref, given_ref, out_ref, psi_ref, half_ref, psi_rest, sent_rest, field, field_rest) = refs[:4], refs[4:13]
     held, arrived = refs[13:17], refs[17]
-    copies = [pltpu.make_async_copy(matrices[i], held[i], arrived.at[i]) for i in range(4)]
+    copies = [pltpu.make_async_copy(matrices[i].at[place_ref[2]], held[i], arrived.at[i]) for i in range(4)]
     for copy in copies:
         copy.start()
     next_ref, next_rest_ref, block_ref, rest_ref = held
     doms, count = blocks_ref.shape[:2]
     size = count * bands
     even = place_ref[1] == 0
-    block = (lax.broadcasted_iota(jnp.int32, (size, LANES), 1) >> 3) & (BLOCKS - 1)
+    block = ((lax.broadcasted_iota(jnp.int32, (size, LANES), 1) >> 3) - place_ref[2]) & (BLOCKS - 1)
     quads = doms // 4
 
     def pair(dom):
         return pl.ds(pl.multiple_of(dom * (2 * LANES), 2 * LANES), 2 * LANES)
 
-    field[...] = 0.5 * decoded(blocks_ref[:, place_ref[0], 3 * bands :, :].astype(jnp.float32)) - 0.75 * STENCIL[0]
+    field[...] = 0.5 * decoded(blocks_ref[:, place_ref[0], 3 * bands :, :].astype(jnp.float32), block) - 0.75 * STENCIL[0]
 
     @pl.loop(0, doms, unroll=2)
     def _(dom):
@@ -342,7 +348,7 @@
             pltpu.VMEM((doms // 4, size, LANES), jnp.float32),
             pltpu.VMEM((doms, 1, 3 * LANES), jnp.float32),
             pltpu.VMEM((doms // 4, 1, LANES), jnp.float32),
-            *[pltpu.VMEM(each.shape, each.dtype) for each in matrices],
+            *[pltpu.VMEM(each.shape[1:], each.dtype) for each in matrices],
             pltpu.SemaphoreType.DMA((4,)),
         ],
         compiler_params=pltpu.CompilerParams(vmem_limit_bytes=32 * 2**20),
@@ -367,6 +373,7 @@
             pltpu.VMEM((layers * bands, cells_row + 2 * cells), jnp.bfloat16),
             pltpu.VMEM((21 * LANES, 2 * LANES), jnp.bfloat16),
             pltpu.VMEM(potential.shape, jnp.float32),
+            pltpu.VMEM((2, 3 * bands + -3 * bands % 16, (group + 2) * cells), jnp.bfloat16),
             pltpu.SemaphoreType.DMA((8,)),
         ],
         compiler_params=pltpu.CompilerParams(vmem_limit_bytes=24 * 2**20),
@@ -381,7 +388,7 @@
     size = count * bands
     cells_all = layers * doms * cells_row
     band, dom = lax.axis_index("band"), lax.axis_index("dom")
-    place = jnp.stack([band, (band + dom) & 1]).astype(jnp.int32)
+    place = jnp.stack([band, (band + dom) & 1, dom]).astype(jnp.int32)
     packed = pack(doms, count, place, orbitals, potential)
     chunk = packed.shape[2]
     received = lax.all_to_all(packed.reshape(doms * count, chunk, LANES), ("dom", "band"), 0, 0, tiled=True)

time: 88 us -> 86.8 us (0.986)
  Pallas kernels: 12.7 us -> 11.4 us
    pallas_call x1, Pallas kernels: 6.74 us -> 5.53 us  [pack(): pl.pallas_call(functools.partial(apply_kernel, layers, bands, rows, group...]
where the time goes in v5:
time: 86.8 us; the launch traced here: 86.5 us
  blocking collectives  72.6 us (84%)
  Pallas kernels  11.4 us (13%)
  waiting for transfers between devices  1.57 us (2%)
    all_to_all x1, blocking collectives, per_device(): lax.all_to_all(packed.reshape(doms * count, chunk, LANES), ('dom', 'band'...  49.8 us
    all_to_all x1, blocking collectives, per_device(): return lax.all_to_all(copies, 'dom', 0, 0, tiled=True).sum(0)  12 us
    all_to_all x1, blocking collectives, per_device(): lax.all_to_all(kept, 'band', 0, 0, axis_index_groups=same_core, tiled=True)  10.8 us
    pallas_call x1, Pallas kernels, project(): pl.pallas_call(functools.partial(product_kernel, bands, scaling), in_spec...  5.9 us
    pallas_call x1, Pallas kernels, pack(): pl.pallas_call(functools.partial(apply_kernel, layers, bands, rows, group...  5.53 us
  transfers between devices with their start and end apart: 1, of which 1 were waited for; matrix products, arithmetic and copies ran while one was open for 0% of the time, Pallas kernels for 0%

profile of v5, /device:TPU:0, one launch (start us, length us, event | category | flops | bytes accessed | tf_op | source)
XLA Modules:
  0.0 86.5 jit_solution(11433399551010854369)
XLA Ops:
  0.0 0.1 pad_add_fusion.place_ref
  0.1 5.5 %apply_upward.1 = bf16[8,16,88,128]{3,2,1,0:T(8,128)(2,1)S(1)} custom-call(s32[3]{0:T(128)S(1)} %pad_add_fusion.place_ref, bf16[144,6144]{1,0:T(8,128)(2,1)} %bitcast.10, bf16[2688,256]{1,0:T(8,128)(2,1)} %constant.23.clone.plane_ref, f32[6,384]{1,0:T(8,128)} %potential_ref.1), custom_call_target="tpu_custom_call" | custom-call | tf_op jit(solution)/shard_map/apply_upward/pallas_call | solution.py:367
  5.6 49.8 %all_to_all.15 = bf16[128,88,128]{2,1,0:T(8,128)(2,1)S(1)} all-to-all(bf16[128,88,128]{2,1,0:T(8,128)(2,1)S(1)} %bitcast.8), channel_id=1, replica_groups=mesh['band'=16,'dom'=8] {'dom','band'}, dimensions={0} | all-to-all | bytes 5767168 | tf_op jit(solution)/shard_map/all_to_all | solution.py:394
  55.4 5.9 %subspace_product.1 = (f32[8,24,384]{2,1,0:T(8,128)S(1)}, f32[8,24,384]{2,1,0:T(8,128)S(1)}) custom-call(s32[3]{0:T(128)S(1)} %pad_add_fusion.place_ref, bf16[8,16,88,128]{3,2,1,0:T(8,128)(2,1)S(1)} %bitcast.9, bf16[8,256,512]{2,1,0:T(8,128)(2,1)} %constant.24.clone.refs_0_, bf16[8,1024,256]{2,1,0:T(8,128)(2,1)} %constant.25.clone.refs_1_, ...), custom_call_target="tpu_custom_call" | custom-call | tf_op jit(solution)/shard_map/subspace_product/pallas_call | solution.py:338
  61.3 0.1 collective-permute-start
  61.4 1.6 %collective-permute-done = f32[8,24,384]{2,1,0:T(8,128)S(1)} collective-permute-done((f32[8,24,384]{2,1,0:T(8,128)S(1)}, f32[8,24,384]{2,1,0:T(8,128)S(1)}, u32[]{:S(2)}, u32[]{:S(2)}) %collective-permute-start) | collective-permute-done | bytes 294944 | tf_op jit(solution)/shard_map/ppermute | solution.py:398
  63.0 10.8 %all_to_all.16 = f32[8,24,384]{2,1,0:T(8,128)S(1)} all-to-all(f32[8,24,384]{2,1,0:T(8,128)S(1)} %add.7), channel_id=1, replica_groups={{0,16,32,48,64,80,96,112},{8,24,40,56,72,88,104,120},{1,17,33,49,65,81,..., dimensions={0} | all-to-all | bytes 589824 | tf_op jit(solution)/shard_map/all_to_all | solution.py:399
  73.9 12.0 %all_to_all.17 = f32[8,24,384]{2,1,0:T(8,128)S(1)} all-to-all(f32[8,24,384]{2,1,0:T(8,128)S(1)} %broadcast_in_dim.3), channel_id=1, replica_groups=mesh['band'=16,'dom'=8] {'dom'}, dimensions={0} | all-to-all | bytes 589824 | tf_op jit(solution)/shard_map/all_to_all | solution.py:401
  85.9 0.6 reduce_sum.19
  (3 shorter events, 0.1 us)
Async XLA Ops:
  61.3 1.7 %collective-permute-start = (f32[8,24,384]{2,1,0:T(8,128)S(1)}, f32[8,24,384]{2,1,0:T(8,128)S(1)}, u32[]{:S(2)}, u32[]{:S(2)}) collective-permute-start(f32[8,24,384]{2,1,0:T(8,128)S(1)} %get-tuple-element.8), channel_id=1, source_target_pairs={{0,8},{8,0},{16,24},{24,16},{32,40},{40,32},{48,56},{56,48},{64,72... | collective-permute-start | bytes 884744 | tf_op jit(solution)/shard_map/ppermute | solution.py:398

commit v6 on v5

--- a/solution.py
+++ b/solution.py
@@ -37,25 +37,40 @@
     return high, low
 
 
-def sent_plane():
-    matrices = []
-    for v, window in enumerate(WINDOWS):
-        matrix = np.zeros(((len(window) + 1) * LANES, LANES))
-        for out in range(LANES):
-            y, z = 2 * v + out // NZ, out % NZ
-            for at, other in enumerate(window):
+def sent_plane(plane_ref):
+    row = lax.broadcasted_iota(jnp.int32, (LANES, LANES), 0)
+    lane = lax.broadcasted_iota(jnp.int32, (LANES, LANES), 1)
+    apart = (row - lane) & (NZ - 1)
+    same_half = (row ^ lane) & NZ == 0
+    same_block = (row ^ lane) & (NZ - WIDTH) == 0
+    parts = [[float(part) for part in halves(np.float64(-0.5 * c))] for c in STENCIL]
+    start = 0
+    for which in range(2):
+        along = jnp.zeros((LANES, LANES), jnp.float32)
+        for k in range(1, REACH + 1):
+            along = jnp.where((apart == k) | (apart == NZ - k), parts[k][which], along)
+        along = jnp.where(same_half, along, 0.0)
+        inside = jnp.where(same_block & (row > lane), along, 0.0)
+        outside = jnp.where(same_block, 0.0, along)
+        columns = slice(which * LANES, (which + 1) * LANES)
+        start = 0
+        for v, window in enumerate(WINDOWS):
+            for other in window:
+                tile = []
                 for half in range(2):
-                    there = 2 * other + half
-                    k = abs(there - y)
-                    if 1 <= k <= REACH and (there > y or there < 0):
-                        matrix[at * LANES + half * NZ + z, out] += -0.5 * STENCIL[k]
-            own, beside = (at * LANES + out // NZ * NZ for at in (window.index(v), len(window)))
-            for k in range(1, REACH + 1):
-                matrix[(own if z % WIDTH + k < WIDTH else beside) + (z + k) % NZ, out] += -0.5 * STENCIL[k]
-                if z % WIDTH - k < 0:
-                    matrix[beside + (z - k) % NZ, out] += -0.5 * STENCIL[k]
-        matrices.append(matrix)
-    return jnp.asarray(np.concatenate(halves(np.concatenate(matrices)), axis=1))
+                    weight = []
+                    for out in range(2):
+                        there, y = 2 * other + half, 2 * v + out
+                        k = abs(there - y)
+                        weight.append(parts[k][which] if 1 <= k <= REACH and (there > y or there < 0) else 0.0)
+                    above = slice(half * NZ, (half + 1) * NZ)
+                    across = jnp.where(lane[above] < NZ, weight[0], weight[1])
+                    part = jnp.where(apart[above] == 0, across, 0.0)
+                    tile.append(part + inside[above] if other == v else part)
+                plane_ref[start : start + LANES, columns] = jnp.concatenate(tile, axis=0).astype(jnp.bfloat16)
+                start += LANES
+            plane_ref[start : start + LANES, columns] = outside.astype(jnp.bfloat16)
+            start += LANES
 
 
 def placed(x, y, j):
@@ -150,7 +165,7 @@
     return jnp.concatenate([jnp.sum(jnp.where(own, part, 0.0), axis=1, keepdims=True) for part in field], axis=2)
 
 
-def apply_kernel(layers, bands, rows, group, place_ref, planes_ref, plane_ref, potential_ref, out_ref, held, plane, potential, spaced, arrived):
+def apply_kernel(layers, bands, rows, group, place_ref, planes_ref, potential_ref, out_ref, held, plane, potential, spaced, arrived):
     size, width = planes_ref.shape
     side, part = rows * LANES, width // 4
     ends = [(width - side, 0, side)] + [(i * part, side + i * part, part) for i in range(4)] + [(0, side + width, side)]
@@ -158,10 +173,11 @@
         pltpu.make_async_copy(planes_ref.at[:, pl.ds(start, count)], held.at[:, pl.ds(end, count)], arrived.at[i])
         for i, (start, end, count) in enumerate(ends)
     ]
-    copies += [pltpu.make_async_copy(plane_ref, plane, arrived.at[6]), pltpu.make_async_copy(potential_ref, potential, arrived.at[7])]
-    for i in (7, 0, 1, 6, 2, 3, 4, 5):
+    copies.append(pltpu.make_async_copy(potential_ref, potential, arrived.at[6]))
+    for i in (6, 0, 1, 2, 3, 4, 5):
         copies[i].start()
-    for i in (7, 0, 1, 6):
+    sent_plane(plane)
+    for i in (6, 0, 1):
         copies[i].wait()
     codes = coded(potential)
     lane = lax.broadcasted_iota(jnp.int32, (BLOCKS, LANES), 1)
@@ -249,6 +265,7 @@
     even = place_ref[1] == 0
     block = ((lax.broadcasted_iota(jnp.int32, (size, LANES), 1) >> 3) - place_ref[2]) & (BLOCKS - 1)
     quads = doms // 4
+    block_short = block.astype(jnp.int16)
 
     def pair(dom):
         return pl.ds(pl.multiple_of(dom * (2 * LANES), 2 * LANES), 2 * LANES)
@@ -261,11 +278,11 @@
         last = blocks_ref[dom, :, 3 * bands :, :].astype(jnp.float32)
         row = field[dom]
         beside = pltpu.roll(last[:, : bands - FOLD], LANES - 4 * WIDTH, 2)
-        last = jnp.concatenate([last, beside], axis=1).reshape(size, LANES)
-        mine = block >> 1 == i
+        last = jnp.concatenate([last, beside], axis=1).reshape(size, LANES).astype(jnp.bfloat16)
+        mine = block_short & 6 == (2 * i).astype(jnp.int16)
         psi_rest[quad] = jnp.where(mine, pltpu.roll(last, 2 * WIDTH * i, 1), psi_rest[quad])
         sent_rest[quad] = jnp.where(mine, pltpu.roll(last, (2 * WIDTH * (i + 7)) & (LANES - 1), 1), sent_rest[quad])
-        field_rest[quad] = jnp.where(mine[:1], pltpu.roll(row[:, 2 * LANES :], 2 * WIDTH * i, 1), field_rest[quad])
+        field_rest[quad] = jnp.where(block[:1] >> 1 == i, pltpu.roll(row[:, 2 * LANES :], 2 * WIDTH * i, 1), field_rest[quad])
         psi_ref[:, pair(dom)] = jnp.concatenate(
             [blocks_ref[dom, :, at * bands : (at + 1) * bands, :].reshape(size, LANES) for at in range(2)], axis=1
         )
@@ -280,7 +297,7 @@
         low, high = psi[:, :LANES], psi[:, LANES:]
         beyond = jnp.dot(psi_ref[:, pair(after)], next_ref[...], preferred_element_type=jnp.float32)
         kept = psi_rest[dom >> 2]
-        kept = jnp.where(even, kept, pltpu.roll(kept, LANES - WIDTH, 1)).astype(jnp.bfloat16)
+        kept = jnp.where(even, kept, pltpu.roll(kept, LANES - WIDTH, 1))
         kept = jnp.concatenate([jnp.where(even, low, high), kept], axis=1)
         rows = pl.ds(pl.multiple_of(i * (2 * LANES), 2 * LANES), 2 * LANES)
         inner = jnp.dot(kept, block_ref[rows, :], preferred_element_type=jnp.float32)
@@ -288,9 +305,8 @@
         sent = blocks_ref[dom, :, 2 * bands : 3 * bands, :].reshape(size, LANES).astype(jnp.float32)
         lead = psi_rest[after >> 2]
         from_here = 2 * (after & 3)
-        lead = pltpu.roll(lead, ((2 - from_here) * WIDTH) & (LANES - 1), 1) * jnp.where(
-            block[:1] == 2, -0.5 * STENCIL[5], 0.0
-        ) + pltpu.roll(lead, ((5 - from_here) * WIDTH) & (LANES - 1), 1) * jnp.where(block[:1] == 5, -0.5 * STENCIL[4], 0.0)
+        lead = [pltpu.roll(lead, ((place - from_here) * WIDTH) & (LANES - 1), 1).astype(jnp.float32) for place in (2, 5)]
+        lead = lead[0] * jnp.where(block[:1] == 2, -0.5 * STENCIL[5], 0.0) + lead[1] * jnp.where(block[:1] == 5, -0.5 * STENCIL[4], 0.0)
         row = field[dom]
         half_low = beyond[:, :LANES] + beyond[:, 2 * LANES : 3 * LANES] + jnp.where(even, inner, sent)
         half_low = half_low + row[:, :LANES] * low.astype(jnp.float32)
@@ -302,16 +318,16 @@
         here, other = psi_rest[quad], psi_rest[(quad + 1) % quads]
         beyond = [psi_ref[:, 2 * ((4 * quad + i + 1) % doms) * LANES :][:, : 2 * LANES] for i in range(4)]
         beyond = jnp.dot(jnp.concatenate(beyond, axis=1), next_rest_ref[...], preferred_element_type=jnp.float32)
-        ends = here.astype(jnp.bfloat16)
-        inner = jnp.dot(ends, rest_ref[...], preferred_element_type=jnp.float32)
+        inner = jnp.dot(here, rest_ref[...], preferred_element_type=jnp.float32)
         inner = inner[:, :LANES] + inner[:, LANES:]
-        after = jnp.where(block >= 6, pltpu.roll(other, 6 * WIDTH, 1), pltpu.roll(here, LANES - 2 * WIDTH, 1))
-        half = beyond[:, :LANES] + beyond[:, LANES:] + field_rest[quad] * here + (-0.5 * STENCIL[6]) * after
-        half = half + pltpu.roll(after, WIDTH, 1) * jnp.where(block[:1] & 1 == 1, -0.5 * STENCIL[3], 0.0)
-        sent = jnp.where(even, pltpu.roll(sent_rest[quad], WIDTH, 1), sent_rest[quad])
+        after = jnp.where(block_short >= 6, pltpu.roll(other, 6 * WIDTH, 1), pltpu.roll(here, LANES - 2 * WIDTH, 1))
+        half = beyond[:, :LANES] + beyond[:, LANES:] + field_rest[quad] * here.astype(jnp.float32)
+        half = half + (-0.5 * STENCIL[6]) * after.astype(jnp.float32)
+        half = half + pltpu.roll(after, WIDTH, 1).astype(jnp.float32) * jnp.where(block[:1] & 1 == 1, -0.5 * STENCIL[3], 0.0)
+        sent = jnp.where(even, pltpu.roll(sent_rest[quad], WIDTH, 1), sent_rest[quad]).astype(jnp.float32)
         half = half + jnp.where(block & 1 == jnp.where(even, 0, 1), inner, sent)
         place = slice((2 * doms + quad) * LANES, (2 * doms + quad + 1) * LANES)
-        psi_ref[:, place] = ends
+        psi_ref[:, place] = here
         half_ref[:, place] = half.astype(jnp.bfloat16)
 
     whole = lax.dot_general(
@@ -344,8 +360,8 @@
             pltpu.VMEM((2, count // 2, bands, size), jnp.float32),
             pltpu.VMEM((size, width), jnp.bfloat16),
             pltpu.VMEM((size, width), jnp.bfloat16),
-            pltpu.VMEM((doms // 4, size, LANES), jnp.float32),
-            pltpu.VMEM((doms // 4, size, LANES), jnp.float32),
+            pltpu.VMEM((doms // 4, size, LANES), jnp.bfloat16),
+            pltpu.VMEM((doms // 4, size, LANES), jnp.bfloat16),
             pltpu.VMEM((doms, 1, 3 * LANES), jnp.float32),
             pltpu.VMEM((doms // 4, 1, LANES), jnp.float32),
             *[pltpu.VMEM(each.shape[1:], each.dtype) for each in matrices],
@@ -363,10 +379,10 @@
     chunk = 3 * bands + FOLD
     group = 4
     planes = jnp.transpose(orbitals, (1, 0, 2)).reshape(layers * bands, cells_row)
-    operands = [pltpu.with_memory_space_constraint(each, pltpu.HBM) for each in (planes, sent_plane(), potential)]
+    operands = [pltpu.with_memory_space_constraint(each, pltpu.HBM) for each in (planes, potential)]
     return pl.pallas_call(
         functools.partial(apply_kernel, layers, bands, rows, group),
-        in_specs=[pl.BlockSpec(memory_space=pltpu.SMEM)] + [pl.BlockSpec(memory_space=pl.ANY)] * 3,
+        in_specs=[pl.BlockSpec(memory_space=pltpu.SMEM)] + [pl.BlockSpec(memory_space=pl.ANY)] * 2,
         out_specs=pl.BlockSpec(memory_space=pltpu.VMEM),
         out_shape=jax.ShapeDtypeStruct((doms, count, chunk, LANES), jnp.bfloat16),
         scratch_shapes=[
@@ -374,7 +390,7 @@
             pltpu.VMEM((21 * LANES, 2 * LANES), jnp.bfloat16),
             pltpu.VMEM(potential.shape, jnp.float32),
             pltpu.VMEM((2, 3 * bands + -3 * bands % 16, (group + 2) * cells), jnp.bfloat16),
-            pltpu.SemaphoreType.DMA((8,)),
+            pltpu.SemaphoreType.DMA((7,)),
         ],
         compiler_params=pltpu.CompilerParams(vmem_limit_bytes=24 * 2**20),
         name="apply_upward",

time: 86.8 us -> 86.3 us (level)
  no operation moved by 1% of the time
where the time goes in v6:
time: 86.3 us; the launch traced here: 86.1 us
  blocking collectives  72.6 us (84%)
  Pallas kernels  11 us (13%)
  waiting for transfers between devices  1.57 us (2%)
    all_to_all x1, blocking collectives, per_device(): lax.all_to_all(packed.reshape(doms * count, chunk, LANES), ('dom', 'band'...  49.8 us
    all_to_all x1, blocking collectives, per_device(): return lax.all_to_all(copies, 'dom', 0, 0, tiled=True).sum(0)  12 us
    all_to_all x1, blocking collectives, per_device(): lax.all_to_all(kept, 'band', 0, 0, axis_index_groups=same_core, tiled=True)  10.8 us
    pallas_call x1, Pallas kernels, project(): pl.pallas_call(functools.partial(product_kernel, bands, scaling), in_spec...  5.86 us
    pallas_call x1, Pallas kernels, pack(): pl.pallas_call(functools.partial(apply_kernel, layers, bands, rows, group...  5.12 us
  transfers between devices with their start and end apart: 1, of which 1 were waited for; matrix products, arithmetic and copies ran while one was open for 0% of the time, Pallas kernels for 0%

profile of v6, /device:TPU:0, one launch (start us, length us, event | category | flops | bytes accessed | tf_op | source)
XLA Modules:
  0.0 86.1 jit_solution(167381473485846206)
XLA Ops:
  0.0 0.1 pad_add_fusion.place_ref
  0.1 5.1 %apply_upward.1 = bf16[8,16,88,128]{3,2,1,0:T(8,128)(2,1)S(1)} custom-call(s32[3]{0:T(128)S(1)} %pad_add_fusion.place_ref, bf16[144,6144]{1,0:T(8,128)(2,1)} %bitcast.10, f32[6,384]{1,0:T(8,128)} %potential_ref.1), custom_call_target="tpu_custom_call" | custom-call | tf_op jit(solution)/shard_map/apply_upward/pallas_call | solution.py:383
  5.2 49.8 %all_to_all.15 = bf16[128,88,128]{2,1,0:T(8,128)(2,1)S(1)} all-to-all(bf16[128,88,128]{2,1,0:T(8,128)(2,1)S(1)} %bitcast.8), channel_id=1, replica_groups=mesh['band'=16,'dom'=8] {'dom','band'}, dimensions={0} | all-to-all | bytes 5767168 | tf_op jit(solution)/shard_map/all_to_all | solution.py:410
  55.0 5.9 %subspace_product.1 = (f32[8,24,384]{2,1,0:T(8,128)S(1)}, f32[8,24,384]{2,1,0:T(8,128)S(1)}) custom-call(s32[3]{0:T(128)S(1)} %pad_add_fusion.place_ref, bf16[8,16,88,128]{3,2,1,0:T(8,128)(2,1)S(1)} %bitcast.9, bf16[8,256,512]{2,1,0:T(8,128)(2,1)} %constant.21.clone.refs_0_, bf16[8,1024,256]{2,1,0:T(8,128)(2,1)} %constant.22.clone.refs_1_, ...), custom_call_target="tpu_custom_call" | custom-call | tf_op jit(solution)/shard_map/subspace_product/pallas_call | solution.py:354
  60.9 0.1 collective-permute-start
  61.0 1.6 %collective-permute-done = f32[8,24,384]{2,1,0:T(8,128)S(1)} collective-permute-done((f32[8,24,384]{2,1,0:T(8,128)S(1)}, f32[8,24,384]{2,1,0:T(8,128)S(1)}, u32[]{:S(2)}, u32[]{:S(2)}) %collective-permute-start) | collective-permute-done | bytes 294944 | tf_op jit(solution)/shard_map/ppermute | solution.py:414
  62.6 10.8 %all_to_all.16 = f32[8,24,384]{2,1,0:T(8,128)S(1)} all-to-all(f32[8,24,384]{2,1,0:T(8,128)S(1)} %add.7), channel_id=1, replica_groups={{0,16,32,48,64,80,96,112},{8,24,40,56,72,88,104,120},{1,17,33,49,65,81,..., dimensions={0} | all-to-all | bytes 589824 | tf_op jit(solution)/shard_map/all_to_all | solution.py:415
  73.4 12.0 %all_to_all.17 = f32[8,24,384]{2,1,0:T(8,128)S(1)} all-to-all(f32[8,24,384]{2,1,0:T(8,128)S(1)} %broadcast_in_dim.3), channel_id=1, replica_groups=mesh['band'=16,'dom'=8] {'dom'}, dimensions={0} | all-to-all | bytes 589824 | tf_op jit(solution)/shard_map/all_to_all | solution.py:417
  85.4 0.6 reduce_sum.19
  (3 shorter events, 0.1 us)
Async XLA Ops:
  60.9 1.7 %collective-permute-start = (f32[8,24,384]{2,1,0:T(8,128)S(1)}, f32[8,24,384]{2,1,0:T(8,128)S(1)}, u32[]{:S(2)}, u32[]{:S(2)}) collective-permute-start(f32[8,24,384]{2,1,0:T(8,128)S(1)} %get-tuple-element.8), channel_id=1, source_target_pairs={{0,8},{8,0},{16,24},{24,16},{32,40},{40,32},{48,56},{56,48},{64,72... | collective-permute-start | bytes 884744 | tf_op jit(solution)/shard_map/ppermute | solution.py:414

commit v7 on v6

--- a/solution.py
+++ b/solution.py
@@ -165,7 +165,8 @@
     return jnp.concatenate([jnp.sum(jnp.where(own, part, 0.0), axis=1, keepdims=True) for part in field], axis=2)
 
 
-def apply_kernel(layers, bands, rows, group, place_ref, planes_ref, potential_ref, out_ref, held, plane, potential, spaced, arrived):
+def apply_kernel(layers, bands, rows, group, place_ref, planes_ref, potential_ref, *refs):
+    matrices, out_ref, brought, (held, plane, potential, spaced, arrived) = refs[:4], refs[4], refs[5:9], refs[9:]
     size, width = planes_ref.shape
     side, part = rows * LANES, width // 4
     ends = [(width - side, 0, side)] + [(i * part, side + i * part, part) for i in range(4)] + [(0, side + width, side)]
@@ -174,7 +175,8 @@
         for i, (start, end, count) in enumerate(ends)
     ]
     copies.append(pltpu.make_async_copy(potential_ref, potential, arrived.at[6]))
-    for i in (6, 0, 1, 2, 3, 4, 5):
+    copies += [pltpu.make_async_copy(matrices[i].at[place_ref[2]], brought[i], arrived.at[7 + i]) for i in range(4)]
+    for i in (6, 0, 1, 2, 3, 4, 5, 7, 8, 9, 10):
         copies[i].start()
     sent_plane(plane)
     for i in (6, 0, 1):
@@ -252,14 +254,13 @@
             for there, tile in enumerate(exchange_blocks(tiles)):
                 out_ref[there, step * group + at] = tile
 
+    for copy in copies[7:]:
+        copy.wait()
+
 
 def product_kernel(bands, scaling, place_ref, blocks_ref, *refs):
-    matrices, (kept_ref, given_ref, out_ref, psi_ref, half_ref, psi_rest, sent_rest, field, field_rest) = refs[:4], refs[4:13]
-    held, arrived = refs[13:17], refs[17]
-    copies = [pltpu.make_async_copy(matrices[i].at[place_ref[2]], held[i], arrived.at[i]) for i in range(4)]
-    for copy in copies:
-        copy.start()
-    next_ref, next_rest_ref, block_ref, rest_ref = held
+    next_ref, next_rest_ref, block_ref, rest_ref = refs[:4]
+    kept_ref, given_ref, out_ref, psi_ref, half_ref, psi_rest, sent_rest, field, field_rest = refs[4:]
     doms, count = blocks_ref.shape[:2]
     size = count * bands
     even = place_ref[1] == 0
@@ -272,7 +273,7 @@
 
     field[...] = 0.5 * decoded(blocks_ref[:, place_ref[0], 3 * bands :, :].astype(jnp.float32), block) - 0.75 * STENCIL[0]
 
-    @pl.loop(0, doms, unroll=2)
+    @pl.loop(0, doms, unroll=8)
     def _(dom):
         quad, i = dom >> 2, dom & 3
         last = blocks_ref[dom, :, 3 * bands :, :].astype(jnp.float32)
@@ -287,10 +288,7 @@
             [blocks_ref[dom, :, at * bands : (at + 1) * bands, :].reshape(size, LANES) for at in range(2)], axis=1
         )
 
-    for copy in copies:
-        copy.wait()
-
-    @pl.loop(0, doms, unroll=2)
+    @pl.loop(0, doms, unroll=8)
     def _(dom):
         i, after = dom & 3, (dom + 1) & (doms - 1)
         psi = psi_ref[:, pair(dom)]
@@ -345,15 +343,14 @@
     given_ref[...] = jnp.where(core == 0, second, first)
 
 
-def project(bands, scaling, layers, place, received):
+def project(bands, scaling, place, received, matrices):
     doms, count, chunk, _ = received.shape
     size = count * bands
     width = (2 * doms + doms // 4) * LANES
     whole = pl.BlockSpec(memory_space=pltpu.VMEM)
-    matrices = [*upward_next(layers), *upward_block()]
     return pl.pallas_call(
         functools.partial(product_kernel, bands, scaling),
-        in_specs=[pl.BlockSpec(memory_space=pltpu.SMEM), whole] + [pl.BlockSpec(memory_space=pl.ANY)] * 4,
+        in_specs=[pl.BlockSpec(memory_space=pltpu.SMEM)] + [whole] * 5,
         out_specs=[whole] * 2,
         out_shape=[jax.ShapeDtypeStruct((count // 2, bands, size), jnp.float32)] * 2,
         scratch_shapes=[
@@ -364,12 +361,10 @@
             pltpu.VMEM((doms // 4, size, LANES), jnp.bfloat16),
             pltpu.VMEM((doms, 1, 3 * LANES), jnp.float32),
             pltpu.VMEM((doms // 4, 1, LANES), jnp.float32),
-            *[pltpu.VMEM(each.shape[1:], each.dtype) for each in matrices],
-            pltpu.SemaphoreType.DMA((4,)),
         ],
         compiler_params=pltpu.CompilerParams(vmem_limit_bytes=32 * 2**20),
         name="subspace_product",
-    )(place, received, *[pltpu.with_memory_space_constraint(each, pltpu.HBM) for each in matrices])
+    )(place, received, *matrices)
 
 
 def pack(doms, count, place, orbitals, potential):
@@ -379,18 +374,20 @@
     chunk = 3 * bands + FOLD
     group = 4
     planes = jnp.transpose(orbitals, (1, 0, 2)).reshape(layers * bands, cells_row)
-    operands = [pltpu.with_memory_space_constraint(each, pltpu.HBM) for each in (planes, potential)]
+    matrices = [*upward_next(layers), *upward_block()]
+    operands = [pltpu.with_memory_space_constraint(each, pltpu.HBM) for each in (planes, potential, *matrices)]
     return pl.pallas_call(
         functools.partial(apply_kernel, layers, bands, rows, group),
-        in_specs=[pl.BlockSpec(memory_space=pltpu.SMEM)] + [pl.BlockSpec(memory_space=pl.ANY)] * 2,
-        out_specs=pl.BlockSpec(memory_space=pltpu.VMEM),
-        out_shape=jax.ShapeDtypeStruct((doms, count, chunk, LANES), jnp.bfloat16),
+        in_specs=[pl.BlockSpec(memory_space=pltpu.SMEM)] + [pl.BlockSpec(memory_space=pl.ANY)] * 6,
+        out_specs=[pl.BlockSpec(memory_space=pltpu.VMEM)] * 5,
+        out_shape=[jax.ShapeDtypeStruct((doms, count, chunk, LANES), jnp.bfloat16)]
+        + [jax.ShapeDtypeStruct(each.shape[1:], each.dtype) for each in matrices],
         scratch_shapes=[
             pltpu.VMEM((layers * bands, cells_row + 2 * cells), jnp.bfloat16),
             pltpu.VMEM((21 * LANES, 2 * LANES), jnp.bfloat16),
             pltpu.VMEM(potential.shape, jnp.float32),
             pltpu.VMEM((2, 3 * bands + -3 * bands % 16, (group + 2) * cells), jnp.bfloat16),
-            pltpu.SemaphoreType.DMA((7,)),
+            pltpu.SemaphoreType.DMA((11,)),
         ],
         compiler_params=pltpu.CompilerParams(vmem_limit_bytes=24 * 2**20),
         name="apply_upward",
@@ -405,10 +402,10 @@
     cells_all = layers * doms * cells_row
     band, dom = lax.axis_index("band"), lax.axis_index("dom")
     place = jnp.stack([band, (band + dom) & 1, dom]).astype(jnp.int32)
-    packed = pack(doms, count, place, orbitals, potential)
+    packed, *matrices = pack(doms, count, place, orbitals, potential)
     chunk = packed.shape[2]
     received = lax.all_to_all(packed.reshape(doms * count, chunk, LANES), ("dom", "band"), 0, 0, tiled=True)
-    kept, given = project(bands, 1.0 / math.sqrt(cells_all), layers, place, received.reshape(doms, count, chunk, LANES))
+    kept, given = project(bands, 1.0 / math.sqrt(cells_all), place, received.reshape(doms, count, chunk, LANES), matrices)
     cores = [(i, i ^ 1) for i in range(count)]
     same_core = [list(range(core, count, 2)) for core in range(2)]
     kept = kept + lax.ppermute(given, "band", cores)

time: 86.3 us -> 85.2 us (0.987)
  Pallas kernels: 11 us -> 9.82 us
    pallas_call x1, Pallas kernels: 5.86 us -> 4.65 us  [project(): pl.pallas_call(functools.partial(product_kernel, bands, scaling), in_spec...]
where the time goes in v7:
time: 85.2 us; the launch traced here: 84.9 us
  blocking collectives  72.6 us (85%)
  Pallas kernels  9.82 us (12%)
  waiting for transfers between devices  1.57 us (2%)
    all_to_all x1, blocking collectives, per_device(): lax.all_to_all(packed.reshape(doms * count, chunk, LANES), ('dom', 'band'...  49.8 us
    all_to_all x1, blocking collectives, per_device(): return lax.all_to_all(copies, 'dom', 0, 0, tiled=True).sum(0)  12 us
    all_to_all x1, blocking collectives, per_device(): lax.all_to_all(kept, 'band', 0, 0, axis_index_groups=same_core, tiled=True)  10.8 us
    pallas_call x1, Pallas kernels, pack(): pl.pallas_call(functools.partial(apply_kernel, layers, bands, rows, group...  5.16 us
    pallas_call x1, Pallas kernels, project(): pl.pallas_call(functools.partial(product_kernel, bands, scaling), in_spec...  4.65 us
  transfers between devices with their start and end apart: 1, of which 1 were waited for; matrix products, arithmetic and copies ran while one was open for 0% of the time, Pallas kernels for 0%

profile of v7, /device:TPU:0, one launch (start us, length us, event | category | flops | bytes accessed | tf_op | source)
XLA Modules:
  0.0 84.9 jit_solution(9333936993015146185)
XLA Ops:
  0.0 0.1 pad_add_fusion.place_ref
  0.1 5.2 %apply_upward.1 = (bf16[8,16,88,128]{3,2,1,0:T(8,128)(2,1)S(1)}, bf16[256,512]{1,0:T(8,128)(2,1)S(1)}, bf16[1024,256]{1,0:T(8,128)(2,1)S(1)}, bf16[1024,256]{1,0:T(8,128)(2,1)S(1)}, bf16[128,256]{1,0:T(8,128)(2,1)S(1)}) custom-call(s32[3]{0:T(128)S(1)} %pad_add_fusion.place_ref, bf16[144,6144]{1,0:T(8,128)(2,1)} %bitcast.10, f32[6,384]{1,0:T(8,128)} %potential_ref.1, ...), custom_call_target="tpu_custom_call" | custom-call | tf_op jit(solution)/shard_map/apply_upward/pallas_call | solution.py:379
  5.2 49.8 %all_to_all.15 = bf16[128,88,128]{2,1,0:T(8,128)(2,1)S(1)} all-to-all(bf16[128,88,128]{2,1,0:T(8,128)(2,1)S(1)} %bitcast.9), channel_id=1, replica_groups=mesh['band'=16,'dom'=8] {'dom','band'}, dimensions={0} | all-to-all | bytes 5767168 | tf_op jit(solution)/shard_map/all_to_all | solution.py:407
  55.0 4.7 %subspace_product.1 = (f32[8,24,384]{2,1,0:T(8,128)S(1)}, f32[8,24,384]{2,1,0:T(8,128)S(1)}) custom-call(s32[3]{0:T(128)S(1)} %pad_add_fusion.place_ref, bf16[8,16,88,128]{3,2,1,0:T(8,128)(2,1)S(1)} %bitcast.8, bf16[256,512]{1,0:T(8,128)(2,1)S(1)} %get-tuple-element.13.refs_0_, bf16[1024,256]{1,0:T(8,128)(2,1)S(1)} %get-tuple-element.14.refs_1_, ...), custom_call_target="tpu_custom_call" | custom-call | tf_op jit(solution)/shard_map/subspace_product/pallas_call | solution.py:351
  59.7 0.1 collective-permute-start
  59.8 1.6 %collective-permute-done = f32[8,24,384]{2,1,0:T(8,128)S(1)} collective-permute-done((f32[8,24,384]{2,1,0:T(8,128)S(1)}, f32[8,24,384]{2,1,0:T(8,128)S(1)}, u32[]{:S(2)}, u32[]{:S(2)}) %collective-permute-start) | collective-permute-done | bytes 294944 | tf_op jit(solution)/shard_map/ppermute | solution.py:411
  61.4 10.8 %all_to_all.16 = f32[8,24,384]{2,1,0:T(8,128)S(1)} all-to-all(f32[8,24,384]{2,1,0:T(8,128)S(1)} %add.7), channel_id=1, replica_groups={{0,16,32,48,64,80,96,112},{8,24,40,56,72,88,104,120},{1,17,33,49,65,81,..., dimensions={0} | all-to-all | bytes 589824 | tf_op jit(solution)/shard_map/all_to_all | solution.py:412
  72.2 12.0 %all_to_all.17 = f32[8,24,384]{2,1,0:T(8,128)S(1)} all-to-all(f32[8,24,384]{2,1,0:T(8,128)S(1)} %broadcast_in_dim.3), channel_id=1, replica_groups=mesh['band'=16,'dom'=8] {'dom'}, dimensions={0} | all-to-all | bytes 589824 | tf_op jit(solution)/shard_map/all_to_all | solution.py:414
  84.3 0.6 reduce_sum.19
  (3 shorter events, 0.1 us)
Async XLA Ops:
  59.7 1.7 %collective-permute-start = (f32[8,24,384]{2,1,0:T(8,128)S(1)}, f32[8,24,384]{2,1,0:T(8,128)S(1)}, u32[]{:S(2)}, u32[]{:S(2)}) collective-permute-start(f32[8,24,384]{2,1,0:T(8,128)S(1)} %get-tuple-element.18), channel_id=1, source_target_pairs={{0,8},{8,0},{16,24},{24,16},{32,40},{40,32},{48,56},{56,48},{64,72... | collective-permute-start | bytes 884744 | tf_op jit(solution)/shard_map/ppermute | solution.py:411

commit v8 on v7

--- a/solution.py
+++ b/solution.py
@@ -269,18 +269,17 @@
     block_short = block.astype(jnp.int16)
 
     def pair(dom):
-        return pl.ds(pl.multiple_of(dom * (2 * LANES), 2 * LANES), 2 * LANES)
+        return slice(dom * 2 * LANES, (dom + 1) * 2 * LANES)
 
     field[...] = 0.5 * decoded(blocks_ref[:, place_ref[0], 3 * bands :, :].astype(jnp.float32), block) - 0.75 * STENCIL[0]
 
-    @pl.loop(0, doms, unroll=8)
-    def _(dom):
+    for dom in range(doms):
         quad, i = dom >> 2, dom & 3
         last = blocks_ref[dom, :, 3 * bands :, :].astype(jnp.float32)
         row = field[dom]
         beside = pltpu.roll(last[:, : bands - FOLD], LANES - 4 * WIDTH, 2)
         last = jnp.concatenate([last, beside], axis=1).reshape(size, LANES).astype(jnp.bfloat16)
-        mine = block_short & 6 == (2 * i).astype(jnp.int16)
+        mine = block_short & 6 == 2 * i
         psi_rest[quad] = jnp.where(mine, pltpu.roll(last, 2 * WIDTH * i, 1), psi_rest[quad])
         sent_rest[quad] = jnp.where(mine, pltpu.roll(last, (2 * WIDTH * (i + 7)) & (LANES - 1), 1), sent_rest[quad])
         field_rest[quad] = jnp.where(block[:1] >> 1 == i, pltpu.roll(row[:, 2 * LANES :], 2 * WIDTH * i, 1), field_rest[quad])
@@ -288,8 +287,7 @@
             [blocks_ref[dom, :, at * bands : (at + 1) * bands, :].reshape(size, LANES) for at in range(2)], axis=1
         )
 
-    @pl.loop(0, doms, unroll=8)
-    def _(dom):
+    def apply(dom):
         i, after = dom & 3, (dom + 1) & (doms - 1)
         psi = psi_ref[:, pair(dom)]
         low, high = psi[:, :LANES], psi[:, LANES:]
@@ -297,7 +295,7 @@
         kept = psi_rest[dom >> 2]
         kept = jnp.where(even, kept, pltpu.roll(kept, LANES - WIDTH, 1))
         kept = jnp.concatenate([jnp.where(even, low, high), kept], axis=1)
-        rows = pl.ds(pl.multiple_of(i * (2 * LANES), 2 * LANES), 2 * LANES)
+        rows = slice(i * 2 * LANES, (i + 1) * 2 * LANES)
         inner = jnp.dot(kept, block_ref[rows, :], preferred_element_type=jnp.float32)
         inner = inner[:, :LANES] + inner[:, LANES:]
         sent = blocks_ref[dom, :, 2 * bands : 3 * bands, :].reshape(size, LANES).astype(jnp.float32)
@@ -311,6 +309,14 @@
         half_high = beyond[:, LANES : 2 * LANES] + beyond[:, 3 * LANES :] + jnp.where(even, sent, inner)
         half_high = half_high + lead + row[:, LANES : 2 * LANES] * high.astype(jnp.float32)
         half_ref[:, pair(dom)] = jnp.concatenate([half_low, half_high], axis=1).astype(jnp.bfloat16)
+
+    for dom in range(doms // 2):
+        apply(dom)
+    early = lax.dot_general(
+        psi_ref[:, : doms * LANES], half_ref[:, : doms * LANES], (((1,), (1,)), ((), ())), preferred_element_type=jnp.float32
+    )
+    for dom in range(doms // 2, doms):
+        apply(dom)
 
     for quad in range(quads):
         here, other = psi_rest[quad], psi_rest[(quad + 1) % quads]
@@ -328,9 +334,12 @@
         psi_ref[:, place] = here
         half_ref[:, place] = half.astype(jnp.bfloat16)
 
-    whole = lax.dot_general(
-        psi_ref[...], half_ref[...], (((1,), (1,)), ((), ())), preferred_element_type=jnp.float32
-    )
+    whole = early
+    for start, end in ((doms, 2 * doms + quads),):
+        place = slice(start * LANES, end * LANES)
+        whole = whole + lax.dot_general(
+            psi_ref[:, place], half_ref[:, place], (((1,), (1,)), ((), ())), preferred_element_type=jnp.float32
+        )
     whole = whole * scaling
     whole = whole + whole.T
     core = place_ref[0] & 1

time: 85.2 us -> 85 us (level)
  no operation moved by 1% of the time
where the time goes in v8:
time: 85 us; the launch traced here: 84.8 us
  blocking collectives  72.6 us (85%)
  Pallas kernels  9.66 us (11%)
  waiting for transfers between devices  1.57 us (2%)
    all_to_all x1, blocking collectives, per_device(): lax.all_to_all(packed.reshape(doms * count, chunk, LANES), ('dom', 'band'...  49.8 us
    all_to_all x1, blocking collectives, per_device(): return lax.all_to_all(copies, 'dom', 0, 0, tiled=True).sum(0)  12 us
    all_to_all x1, blocking collectives, per_device(): lax.all_to_all(kept, 'band', 0, 0, axis_index_groups=same_core, tiled=True)  10.8 us
    pallas_call x1, Pallas kernels, pack(): pl.pallas_call(functools.partial(apply_kernel, layers, bands, rows, group...  5.16 us
    pallas_call x1, Pallas kernels, project(): pl.pallas_call(functools.partial(product_kernel, bands, scaling), in_spec...  4.5 us
  transfers between devices with their start and end apart: 1, of which 1 were waited for; matrix products, arithmetic and copies ran while one was open for 0% of the time, Pallas kernels for 0%

profile of v8, /device:TPU:0, one launch (start us, length us, event | category | flops | bytes accessed | tf_op | source)
XLA Modules:
  0.0 84.8 jit_solution(8179771001654396914)
XLA Ops:
  0.0 0.1 pad_add_fusion.place_ref
  0.1 5.2 %apply_upward.1 = (bf16[8,16,88,128]{3,2,1,0:T(8,128)(2,1)S(1)}, bf16[256,512]{1,0:T(8,128)(2,1)S(1)}, bf16[1024,256]{1,0:T(8,128)(2,1)S(1)}, bf16[1024,256]{1,0:T(8,128)(2,1)S(1)}, bf16[128,256]{1,0:T(8,128)(2,1)S(1)}) custom-call(s32[3]{0:T(128)S(1)} %pad_add_fusion.place_ref, bf16[144,6144]{1,0:T(8,128)(2,1)} %bitcast.10, f32[6,384]{1,0:T(8,128)} %potential_ref.1, ...), custom_call_target="tpu_custom_call" | custom-call | tf_op jit(solution)/shard_map/apply_upward/pallas_call | solution.py:388
  5.2 49.8 %all_to_all.15 = bf16[128,88,128]{2,1,0:T(8,128)(2,1)S(1)} all-to-all(bf16[128,88,128]{2,1,0:T(8,128)(2,1)S(1)} %bitcast.9), channel_id=1, replica_groups=mesh['band'=16,'dom'=8] {'dom','band'}, dimensions={0} | all-to-all | bytes 5767168 | tf_op jit(solution)/shard_map/all_to_all | solution.py:416
  55.0 4.5 %subspace_product.1 = (f32[8,24,384]{2,1,0:T(8,128)S(1)}, f32[8,24,384]{2,1,0:T(8,128)S(1)}) custom-call(s32[3]{0:T(128)S(1)} %pad_add_fusion.place_ref, bf16[8,16,88,128]{3,2,1,0:T(8,128)(2,1)S(1)} %bitcast.8, bf16[256,512]{1,0:T(8,128)(2,1)S(1)} %get-tuple-element.13.refs_0_, bf16[1024,256]{1,0:T(8,128)(2,1)S(1)} %get-tuple-element.14.refs_1_, ...), custom_call_target="tpu_custom_call" | custom-call | tf_op jit(solution)/shard_map/subspace_product/pallas_call | solution.py:360
  59.5 0.1 collective-permute-start
  59.6 1.6 %collective-permute-done = f32[8,24,384]{2,1,0:T(8,128)S(1)} collective-permute-done((f32[8,24,384]{2,1,0:T(8,128)S(1)}, f32[8,24,384]{2,1,0:T(8,128)S(1)}, u32[]{:S(2)}, u32[]{:S(2)}) %collective-permute-start) | collective-permute-done | bytes 294944 | tf_op jit(solution)/shard_map/ppermute | solution.py:420
  61.2 10.8 %all_to_all.16 = f32[8,24,384]{2,1,0:T(8,128)S(1)} all-to-all(f32[8,24,384]{2,1,0:T(8,128)S(1)} %add.7), channel_id=1, replica_groups={{0,16,32,48,64,80,96,112},{8,24,40,56,72,88,104,120},{1,17,33,49,65,81,..., dimensions={0} | all-to-all | bytes 589824 | tf_op jit(solution)/shard_map/all_to_all | solution.py:421
  72.1 12.0 %all_to_all.17 = f32[8,24,384]{2,1,0:T(8,128)S(1)} all-to-all(f32[8,24,384]{2,1,0:T(8,128)S(1)} %broadcast_in_dim.3), channel_id=1, replica_groups=mesh['band'=16,'dom'=8] {'dom'}, dimensions={0} | all-to-all | bytes 589824 | tf_op jit(solution)/shard_map/all_to_all | solution.py:423
  84.1 0.6 reduce_sum.19
  (3 shorter events, 0.1 us)
Async XLA Ops:
  59.5 1.7 %collective-permute-start = (f32[8,24,384]{2,1,0:T(8,128)S(1)}, f32[8,24,384]{2,1,0:T(8,128)S(1)}, u32[]{:S(2)}, u32[]{:S(2)}) collective-permute-start(f32[8,24,384]{2,1,0:T(8,128)S(1)} %get-tuple-element.18), channel_id=1, source_target_pairs={{0,8},{8,0},{16,24},{24,16},{32,40},{40,32},{48,56},{56,48},{64,72... | collective-permute-start | bytes 884744 | tf_op jit(solution)/shard_map/ppermute | solution.py:420

commit v9 on v8

--- a/solution.py
+++ b/solution.py
@@ -258,12 +258,16 @@
         copy.wait()
 
 
-def product_kernel(bands, scaling, place_ref, blocks_ref, *refs):
+def either(first, one, other):
+    return one if first else other
+
+
+def product_of(odd, bands, scaling, place_ref, blocks_ref, *refs):
     next_ref, next_rest_ref, block_ref, rest_ref = refs[:4]
     kept_ref, given_ref, out_ref, psi_ref, half_ref, psi_rest, sent_rest, field, field_rest = refs[4:]
     doms, count = blocks_ref.shape[:2]
     size = count * bands
-    even = place_ref[1] == 0
+    even = odd == 0
     block = ((lax.broadcasted_iota(jnp.int32, (size, LANES), 1) >> 3) - place_ref[2]) & (BLOCKS - 1)
     quads = doms // 4
     block_short = block.astype(jnp.int16)
@@ -293,8 +297,8 @@
         low, high = psi[:, :LANES], psi[:, LANES:]
         beyond = jnp.dot(psi_ref[:, pair(after)], next_ref[...], preferred_element_type=jnp.float32)
         kept = psi_rest[dom >> 2]
-        kept = jnp.where(even, kept, pltpu.roll(kept, LANES - WIDTH, 1))
-        kept = jnp.concatenate([jnp.where(even, low, high), kept], axis=1)
+        kept = either(even, kept, pltpu.roll(kept, LANES - WIDTH, 1))
+        kept = jnp.concatenate([either(even, low, high), kept], axis=1)
         rows = slice(i * 2 * LANES, (i + 1) * 2 * LANES)
         inner = jnp.dot(kept, block_ref[rows, :], preferred_element_type=jnp.float32)
         inner = inner[:, :LANES] + inner[:, LANES:]
@@ -304,9 +308,9 @@
         lead = [pltpu.roll(lead, ((place - from_here) * WIDTH) & (LANES - 1), 1).astype(jnp.float32) for place in (2, 5)]
         lead = lead[0] * jnp.where(block[:1] == 2, -0.5 * STENCIL[5], 0.0) + lead[1] * jnp.where(block[:1] == 5, -0.5 * STENCIL[4], 0.0)
         row = field[dom]
-        half_low = beyond[:, :LANES] + beyond[:, 2 * LANES : 3 * LANES] + jnp.where(even, inner, sent)
+        half_low = beyond[:, :LANES] + beyond[:, 2 * LANES : 3 * LANES] + either(even, inner, sent)
         half_low = half_low + row[:, :LANES] * low.astype(jnp.float32)
-        half_high = beyond[:, LANES : 2 * LANES] + beyond[:, 3 * LANES :] + jnp.where(even, sent, inner)
+        half_high = beyond[:, LANES : 2 * LANES] + beyond[:, 3 * LANES :] + either(even, sent, inner)
         half_high = half_high + lead + row[:, LANES : 2 * LANES] * high.astype(jnp.float32)
         half_ref[:, pair(dom)] = jnp.concatenate([half_low, half_high], axis=1).astype(jnp.bfloat16)
 
@@ -328,8 +332,8 @@
         half = beyond[:, :LANES] + beyond[:, LANES:] + field_rest[quad] * here.astype(jnp.float32)
         half = half + (-0.5 * STENCIL[6]) * after.astype(jnp.float32)
         half = half + pltpu.roll(after, WIDTH, 1).astype(jnp.float32) * jnp.where(block[:1] & 1 == 1, -0.5 * STENCIL[3], 0.0)
-        sent = jnp.where(even, pltpu.roll(sent_rest[quad], WIDTH, 1), sent_rest[quad]).astype(jnp.float32)
-        half = half + jnp.where(block & 1 == jnp.where(even, 0, 1), inner, sent)
+        sent = either(even, pltpu.roll(sent_rest[quad], WIDTH, 1), sent_rest[quad]).astype(jnp.float32)
+        half = half + jnp.where(block & 1 == either(even, 0, 1), inner, sent)
         place = slice((2 * doms + quad) * LANES, (2 * doms + quad + 1) * LANES)
         psi_ref[:, place] = here
         half_ref[:, place] = half.astype(jnp.bfloat16)
@@ -350,6 +354,14 @@
     first, second = out_ref[0], out_ref[1]
     kept_ref[...] = jnp.where(core == 0, first, second)
     given_ref[...] = jnp.where(core == 0, second, first)
+
+
+def product_kernel(bands, scaling, place_ref, *refs):
+    for odd in range(2):
+
+        @pl.when(place_ref[1] == odd)
+        def _():
+            product_of(odd, bands, scaling, place_ref, *refs)
 
 
 def project(bands, scaling, place, received, matrices):

time: 85 us -> 85 us (level)
  no operation moved by 1% of the time
where the time goes in v9:
time: 85 us; the launch traced here: 84.7 us
  blocking collectives  72.7 us (86%)
  Pallas kernels  9.57 us (11%)
  waiting for transfers between devices  1.57 us (2%)
    all_to_all x1, blocking collectives, per_device(): lax.all_to_all(packed.reshape(doms * count, chunk, LANES), ('dom', 'band'...  49.8 us
    all_to_all x1, blocking collectives, per_device(): return lax.all_to_all(copies, 'dom', 0, 0, tiled=True).sum(0)  12.1 us
    all_to_all x1, blocking collectives, per_device(): lax.all_to_all(kept, 'band', 0, 0, axis_index_groups=same_core, tiled=True)  10.8 us
    pallas_call x1, Pallas kernels, pack(): pl.pallas_call(functools.partial(apply_kernel, layers, bands, rows, group...  5.16 us
    pallas_call x1, Pallas kernels, project(): pl.pallas_call(functools.partial(product_kernel, bands, scaling), in_spec...  4.4 us
  transfers between devices with their start and end apart: 1, of which 1 were waited for; matrix products, arithmetic and copies ran while one was open for 0% of the time, Pallas kernels for 0%

profile of v9, /device:TPU:0, one launch (start us, length us, event | category | flops | bytes accessed | tf_op | source)
XLA Modules:
  0.0 84.7 jit_solution(10636079773483320932)
XLA Ops:
  0.0 0.1 pad_add_fusion.place_ref
  0.1 5.2 %apply_upward.1 = (bf16[8,16,88,128]{3,2,1,0:T(8,128)(2,1)S(1)}, bf16[256,512]{1,0:T(8,128)(2,1)S(1)}, bf16[1024,256]{1,0:T(8,128)(2,1)S(1)}, bf16[1024,256]{1,0:T(8,128)(2,1)S(1)}, bf16[128,256]{1,0:T(8,128)(2,1)S(1)}) custom-call(s32[3]{0:T(128)S(1)} %pad_add_fusion.place_ref, bf16[144,6144]{1,0:T(8,128)(2,1)} %bitcast.10, f32[6,384]{1,0:T(8,128)} %potential_ref.1, ...), custom_call_target="tpu_custom_call" | custom-call | tf_op jit(solution)/shard_map/apply_upward/pallas_call | solution.py:400
  5.2 49.8 %all_to_all.15 = bf16[128,88,128]{2,1,0:T(8,128)(2,1)S(1)} all-to-all(bf16[128,88,128]{2,1,0:T(8,128)(2,1)S(1)} %bitcast.9), channel_id=1, replica_groups=mesh['band'=16,'dom'=8] {'dom','band'}, dimensions={0} | all-to-all | bytes 5767168 | tf_op jit(solution)/shard_map/all_to_all | solution.py:428
  55.0 4.4 %subspace_product.1 = (f32[8,24,384]{2,1,0:T(8,128)S(1)}, f32[8,24,384]{2,1,0:T(8,128)S(1)}) custom-call(s32[3]{0:T(128)S(1)} %pad_add_fusion.place_ref, bf16[8,16,88,128]{3,2,1,0:T(8,128)(2,1)S(1)} %bitcast.8, bf16[256,512]{1,0:T(8,128)(2,1)S(1)} %get-tuple-element.13.refs_1_, bf16[1024,256]{1,0:T(8,128)(2,1)S(1)} %get-tuple-element.14.refs_2_, ...), custom_call_target="tpu_custom_call" | custom-call | tf_op jit(solution)/shard_map/subspace_product/pallas_call | solution.py:372
  59.4 0.1 collective-permute-start
  59.5 1.6 %collective-permute-done = f32[8,24,384]{2,1,0:T(8,128)S(1)} collective-permute-done((f32[8,24,384]{2,1,0:T(8,128)S(1)}, f32[8,24,384]{2,1,0:T(8,128)S(1)}, u32[]{:S(2)}, u32[]{:S(2)}) %collective-permute-start) | collective-permute-done | bytes 294944 | tf_op jit(solution)/shard_map/ppermute | solution.py:432
  61.1 10.8 %all_to_all.16 = f32[8,24,384]{2,1,0:T(8,128)S(1)} all-to-all(f32[8,24,384]{2,1,0:T(8,128)S(1)} %add.7), channel_id=1, replica_groups={{0,16,32,48,64,80,96,112},{8,24,40,56,72,88,104,120},{1,17,33,49,65,81,..., dimensions={0} | all-to-all | bytes 589824 | tf_op jit(solution)/shard_map/all_to_all | solution.py:433
  72.0 12.1 %all_to_all.17 = f32[8,24,384]{2,1,0:T(8,128)S(1)} all-to-all(f32[8,24,384]{2,1,0:T(8,128)S(1)} %broadcast_in_dim.3), channel_id=1, replica_groups=mesh['band'=16,'dom'=8] {'dom'}, dimensions={0} | all-to-all | bytes 589824 | tf_op jit(solution)/shard_map/all_to_all | solution.py:435
  84.1 0.6 reduce_sum.19
  (3 shorter events, 0.1 us)
Async XLA Ops:
  59.4 1.7 %collective-permute-start = (f32[8,24,384]{2,1,0:T(8,128)S(1)}, f32[8,24,384]{2,1,0:T(8,128)S(1)}, u32[]{:S(2)}, u32[]{:S(2)}) collective-permute-start(f32[8,24,384]{2,1,0:T(8,128)S(1)} %get-tuple-element.18), channel_id=1, source_target_pairs={{0,8},{8,0},{16,24},{24,16},{32,40},{40,32},{48,56},{56,48},{64,72... | collective-permute-start | bytes 884744 | tf_op jit(solution)/shard_map/ppermute | solution.py:432
